TPU v7x, 128 devices: a whole 4x4x4 slice. The times are simulated.
128 devices in a mesh: gx: 8 (over x, y_hi), gy: 16 (over z, y_lo, core).
Axes of the slice: x: 4, y: 4 (y_hi: 2, y_lo: 2; y = y_hi * 2 + y_lo), z: 4, core: 2. Of those that a mesh axis runs over, the one named last changes fastest.
Arguments:
- ensemble: bfloat16 [128, 512, 48, 128], P('gx', 'gy'), may hold values from -6 to 6
- obs_cell: int32 [8, 16, 2048], P('gx', 'gy'), may hold values from 0 to 24575
- obs_value: float32 [8, 16, 2048], P('gx', 'gy'), may hold values from -8 to 8
- obs_weight: float32 [8, 16, 2048], P('gx', 'gy'), may hold values from 0.05 to 0.5
- obs_count: int32 [8, 16], replicated, may hold values from 1 to 2048, as said below
Outputs:
- analysis: bfloat16 [128, 512, 48, 128], P('gx', 'gy')
Inputs may be any that keep to these rules, and one draw needn't show every extreme that they name: `obs_cell`: each observation lies in its own block's cells. `obs_count`: some block has all 2048 slots live.
All inputs are finite; a program needn't handle non-finite values.
Results may differ from a plain program's by a relative error of at most 0.007.
Values may be sent and summed in bfloat16 or wider, within the bound.
A program may use at most 128 MiB of HBM per device.

v0:
```python
import jax
import jax.numpy as jnp
from jax import lax
from jax.experimental import pallas as pl
from jax.experimental.pallas import tpu as pltpu
from jax.sharding import PartitionSpec as P

K = 128
CX = 16
CY = 32
LEV = 48
ROWS = CX * CY * LEV
XROWS = CY * LEV
OBS = 2048
NEWTON = 6
ITERS = 2
PACK = 72
QUART = 256
GROUP = 4

MESH = pl.DeviceIdType.MESH
F32 = jnp.float32
BF16 = jnp.bfloat16
STAT_STEPS = (-2, -1, 1, 2)
STAT_WEIGHTS = (0.5, 0.75, 0.75, 0.5)
BLEND_STEPS = tuple((a, b) for a in (-1, 0, 1) for b in (-1, 0, 1) if (a, b) != (0, 0))


def slot_of(a, b):
    return (a + 1) * 3 + (b + 1)


def mm(a, b):
    return jnp.dot(a, b, preferred_element_type=F32)


def mm_nt(a, b):
    return lax.dot_general(a, b, (((1,), (1,)), ((), ())), preferred_element_type=F32)


def split(x):
    high = x.astype(BF16)
    low = (x - high.astype(F32)).astype(BF16)
    return high, low


def wide(x):
    high, low = split(x)
    return jnp.concatenate([high, low], axis=1)


def times(a, b):
    both = wide(b)
    out = mm(wide(a), jnp.concatenate([both, both], axis=0))
    return out[:, :K] + out[:, K:]


def iotas(shape):
    return lax.broadcasted_iota(jnp.int32, shape, 0), lax.broadcasted_iota(jnp.int32, shape, 1)


def centring():
    row, col = iotas((K, K))
    return jnp.where(row == col, (K - 1.0) / K, -1.0 / K).astype(BF16)


def pack_stats(total):
    half = K // 2
    row, lane = iotas((half, K))
    top = total[:half]
    turned = pltpu.roll(total[half:K], half, 1)
    body = jnp.where(lane < row, turned, top)
    diagonal = jnp.sum(jnp.where(lane == row, turned, 0.0), axis=0, keepdims=True)
    tail_row, _ = iotas((8, K))
    projected = total[K : K + 1]
    tail = jnp.where(tail_row == 0, diagonal, projected)
    return jnp.concatenate([body, tail], axis=0)


def unpack_stats(packed):
    half = K // 2
    row, lane = iotas((half, K))
    body = packed[:half]
    diagonal = packed[half : half + 1]
    projected = packed[half + 1 : half + 2]
    flipped = jnp.concatenate([body, jnp.zeros((half, K), F32)], axis=0).T
    top = jnp.where(lane < row, flipped[:half], body)
    lower = jnp.where(lane < row, body, jnp.where(lane == row, diagonal, flipped[:half]))
    bottom = jnp.where(lane < half, flipped[half:], pltpu.roll(lower, half, 1))
    return jnp.concatenate([top, bottom], axis=0), projected


def transposed_transform(packed):
    gram, projected = unpack_stats(packed)
    row, col = iotas((K, K))
    identity = jnp.where(row == col, 1.0, 0.0).astype(F32)
    system = gram + (K - 1) * identity
    squares = jnp.sum(system * system, axis=0, keepdims=True)
    frobenius = jnp.sqrt(jnp.sum(squares, axis=1, keepdims=True))
    root = system / frobenius
    carried = jnp.broadcast_to(projected, (16, K))
    correction = 1.5 * identity - 0.5 * root
    out = times(jnp.concatenate([root, carried], axis=0), correction)
    root, carried, inverse = out[:K], out[K:], correction
    for step in range(1, NEWTON):
        correction = 1.5 * identity - 0.5 * times(inverse, root)
        if step < NEWTON - 1:
            out = times(jnp.concatenate([inverse, carried, root], axis=0), correction)
            root = out[K + 16 :]
        else:
            out = times(jnp.concatenate([inverse, carried], axis=0), correction)
        inverse, carried = out[:K], out[K : K + 16]
    weights = times(carried, inverse)[0:1] / frobenius
    return (weights + jnp.sqrt((K - 1) / frobenius) * inverse).astype(BF16)


def hats(position):
    below = jnp.maximum(0.0, 0.5 - position)
    above = jnp.maximum(0.0, position - 0.5)
    return below, 1.0 - below - above, above


def hat_of(j, count):
    position = (j + 0.5) / count
    below, above = max(0.0, 0.5 - position), max(0.0, position - 0.5)
    return below, 1.0 - below - above, above


def apply_column(i, matrix_ref, read, write):
    position = (i.astype(F32) + 0.5) / CX
    weights = hats(position)
    sides = []
    for b in range(3):
        blend = weights[0] * matrix_ref[b * K : (b + 1) * K]
        for a in (1, 2):
            at = (a * 3 + b) * K
            blend = blend + weights[a] * matrix_ref[at : at + K]
        sides.append(wide(blend))
    for half in range(2):
        stationary = jnp.concatenate([sides[half], sides[half + 1]], axis=0)
        for group in range(CY // 2 // GROUP):
            first = half * (CY // 2) + group * GROUP
            block = read(first * LEV, GROUP * LEV)
            out = mm_nt(jnp.concatenate([block, block], axis=1), stationary)
            parts = []
            for j in range(GROUP):
                hat = hat_of(first + j, CY)
                piece = out[j * LEV : (j + 1) * LEV]
                parts.append(hat[half] * piece[:, :K] + hat[half + 1] * piece[:, K:])
            write(first * LEV, GROUP * LEV, jnp.concatenate(parts, axis=0).astype(BF16))


def full_matrices(transforms):
    return mm(transforms, centring()) + 1.0 / K


def first_kernel(
    count_ref, cell_ref, cells_ref, value_ref, weight_ref, ens_ref,
    next_ref, blend_ref,
    ens, ens32, picked, rows, matrices, matrices2, stat_x, stat_y, got_x, got_y, nearby,
    load_sem, store_sem, send_x, recv_x, send_y, recv_y, send_t, recv_t,
):
    gx, gy = lax.axis_index("gx"), lax.axis_index("gy")
    nx, ny = lax.axis_size("gx"), lax.axis_size("gy")

    def at(a, b):
        return (lax.rem(gx + a + nx, nx), lax.rem(gy + b + ny, ny))

    partners = [(s, 0) for s in STAT_STEPS] + [(0, s) for s in STAT_STEPS]
    partners += [(a, b) for a in (-1, 1) for b in (-1, 1)]
    barrier = pltpu.get_barrier_semaphore()
    for a, b in partners:
        pl.semaphore_signal(barrier, inc=1, device_id=at(a, b), device_id_type=MESH)

    def column(ref, i):
        return ref.at[pl.ds(pl.multiple_of(i * XROWS, XROWS), XROWS)]

    @pl.loop(0, CX)
    def _(i):
        pltpu.make_async_copy(column(ens_ref, i), column(ens, i), load_sem.at[i]).start()

    count = count_ref[gx, gy]
    cells = cells_ref[...].astype(F32)
    slot = lax.broadcasted_iota(jnp.int32, (1, OBS), 1)
    rows[0:1] = jnp.where(slot < count, weight_ref[...], 0.0)
    rows[1:2] = value_ref[...]
    east = jnp.floor((cells + 0.5) * (1.0 / XROWS))
    north = jnp.floor((cells - XROWS * east + 0.5) * (1.0 / LEV))
    for first, hat in ((2, hats((east + 0.5) / CX)), (5, hats((north + 0.5) / CY))):
        for k in range(3):
            rows[first + k : first + k + 1] = hat[k]

    @pl.loop(0, CX)
    def _(i):
        pltpu.make_async_copy(column(ens_ref, i), column(ens, i), load_sem.at[i]).wait()
        start = pl.multiple_of(i * XROWS, XROWS)
        ens32[pl.ds(start, XROWS)] = ens[pl.ds(start, XROWS)].astype(F32)

    @pl.loop(0, OBS // 16)
    def _(g):
        for r in range(16):
            o = g * 16 + r
            picked[pl.ds(o, 1)] = ens32[pl.ds(cell_ref[0, o], 1)]

    def accumulate(total, q, deviation, centre):
        lanes = slice(q * QUART, (q + 1) * QUART)
        scale, value = rows[0:1, lanes], rows[1:2, lanes]
        anomaly = (scale * deviation).astype(BF16)
        innovation = jnp.broadcast_to(scale * (value - centre), (16, QUART)).astype(BF16)
        return total + mm_nt(jnp.concatenate([anomaly, innovation], axis=0), anomaly)

    def exchange(t, sent, got, send_sem, recv_sem, shift):
        copies = []
        for k, step in enumerate(STAT_STEPS):
            there = STAT_STEPS.index(-step)
            copies.append(
                pltpu.make_async_remote_copy(
                    src_ref=sent.at[t],
                    dst_ref=got.at[t, there],
                    send_sem=send_sem.at[t, k],
                    recv_sem=recv_sem.at[t, there],
                    device_id=at(*shift(step)),
                    device_id_type=MESH,
                )
            )
        return copies

    def finish(copies):
        for copy in copies:
            copy.wait_recv()
        for copy in copies:
            copy.wait_send()

    def weighted(t, sent, got):
        total = sent[t]
        for k in range(4):
            total = total + STAT_WEIGHTS[k] * got[t, k]
        return total

    def apply_some(first, last):
        @pl.loop(first, last)
        def _(i):
            base = i * XROWS

            def read(start, size):
                return ens[pl.ds(pl.multiple_of(base + start, 16), size)]

            def write(start, size, value):
                ens[pl.ds(pl.multiple_of(base + start, 16), size)] = value

            apply_column(i, matrices, read, write)
            pltpu.make_async_copy(column(ens, i), column(next_ref, i), store_sem.at[i]).start()

    for t in range(ITERS):
        total = jnp.zeros((K + 16, K), F32)
        if t == 0:
            row, col = iotas((K + 16, K))
            centre_rows = jnp.where(row == col, (K - 1.0) / K, jnp.where(row < K, -1.0 / K, 1.0 / K))
            centre_rows = centre_rows.astype(BF16)
            for q in range(OBS // QUART):
                block = picked[q * QUART : (q + 1) * QUART].astype(BF16)
                moved = mm_nt(centre_rows, block)
                total = accumulate(total, q, moved[:K], moved[K : K + 1])
        else:
            matrices2[...] = wide(matrices[...])
            for q in range(OBS // QUART):
                lanes = slice(q * QUART, (q + 1) * QUART)
                block = picked[q * QUART : (q + 1) * QUART].astype(BF16)
                block = jnp.concatenate([block, block], axis=1)
                fresh = jnp.zeros((K, QUART), F32)
                for a in range(3):
                    out = mm_nt(matrices2[a * 3 * K : (a + 1) * 3 * K], block)
                    part = rows[5:6, lanes] * out[:K]
                    part = part + rows[6:7, lanes] * out[K : 2 * K]
                    part = part + rows[7:8, lanes] * out[2 * K :]
                    fresh = fresh + rows[2 + a : 3 + a, lanes] * part
                fresh = fresh.astype(BF16).astype(F32)
                centre = jnp.sum(fresh, axis=0, keepdims=True) * (1.0 / K)
                total = accumulate(total, q, fresh - centre, centre)
        stat_x[t] = pack_stats(total)

        if t == 0:
            pl.semaphore_wait(barrier, len(partners))
        copies = exchange(t, stat_x, got_x, send_x, recv_x, lambda step: (step, 0))
        for copy in copies:
            copy.start()
        if t == 1:
            apply_some(0, 5)
        finish(copies)
        stat_y[t] = weighted(t, stat_x, got_x)
        copies = exchange(t, stat_y, got_y, send_y, recv_y, lambda step: (0, step))
        for copy in copies:
            copy.start()
        if t == 1:
            apply_some(5, 10)
        finish(copies)
        own = slot_of(0, 0) * K
        nearby[t, own : own + K] = transposed_transform(weighted(t, stat_y, got_y))
        copies = []
        for k, (a, b) in enumerate(BLEND_STEPS):
            there = slot_of(-a, -b)
            copies.append(
                pltpu.make_async_remote_copy(
                    src_ref=nearby.at[t, pl.ds(own, K)],
                    dst_ref=nearby.at[t, pl.ds(there * K, K)],
                    send_sem=send_t.at[t, k],
                    recv_sem=recv_t.at[t, there],
                    device_id=at(a, b),
                    device_id_type=MESH,
                )
            )
        for copy in copies:
            copy.start()
        if t == 1:
            apply_some(10, 16)
        finish(copies)
        if t == 0:
            matrices[...] = full_matrices(nearby[t])

    blend_ref[...] = nearby[1]

    @pl.loop(0, CX)
    def _(i):
        pltpu.make_async_copy(column(ens, i), column(next_ref, i), store_sem.at[i]).wait()


def last_kernel(blend_ref, ens_ref, out_ref, matrices):
    i = pl.program_id(0)

    @pl.when(i == 0)
    def _():
        matrices[...] = full_matrices(blend_ref[...])

    def read(start, size):
        return ens_ref[start : start + size]

    def write(start, size, value):
        out_ref[start : start + size] = value

    apply_column(i, matrices, read, write)


def shards(ensemble, obs_cell, obs_value, obs_weight, obs_count):
    flat = ensemble.reshape(ROWS, K)
    cells = obs_cell.reshape(1, OBS)
    vmem = pl.BlockSpec(memory_space=pltpu.VMEM)
    smem = pl.BlockSpec(memory_space=pltpu.SMEM)
    anywhere = pl.BlockSpec(memory_space=pl.ANY)
    dma = pltpu.SemaphoreType.DMA
    following, blend = pl.pallas_call(
        first_kernel,
        out_shape=(
            jax.ShapeDtypeStruct((ROWS, K), BF16),
            jax.ShapeDtypeStruct((9 * K, K), BF16),
        ),
        in_specs=[smem, smem, vmem, vmem, vmem, anywhere],
        out_specs=(anywhere, vmem),
        scratch_shapes=[
            pltpu.VMEM((ROWS, K), BF16),
            pltpu.VMEM((ROWS, K), F32),
            pltpu.VMEM((OBS, K), F32),
            pltpu.VMEM((8, OBS), F32),
            pltpu.VMEM((9 * K, K), F32),
            pltpu.VMEM((9 * K, 2 * K), BF16),
            pltpu.VMEM((ITERS, PACK, K), F32),
            pltpu.VMEM((ITERS, PACK, K), F32),
            pltpu.VMEM((ITERS, 4, PACK, K), F32),
            pltpu.VMEM((ITERS, 4, PACK, K), F32),
            pltpu.VMEM((ITERS, 9 * K, K), BF16),
            dma((CX,)),
            dma((CX,)),
            dma((ITERS, 4)),
            dma((ITERS, 4)),
            dma((ITERS, 4)),
            dma((ITERS, 4)),
            dma((ITERS, 8)),
            dma((ITERS, 9)),
        ],
        compiler_params=pltpu.CompilerParams(
            collective_id=0, has_side_effects=True, vmem_limit_bytes=40 * 1024 * 1024
        ),
        name="analyse",
    )(obs_count, cells, cells, obs_value.reshape(1, OBS), obs_weight.reshape(1, OBS), flat)
    out = pl.pallas_call(
        last_kernel,
        grid=(CX,),
        out_shape=jax.ShapeDtypeStruct((ROWS, K), BF16),
        in_specs=[
            pl.BlockSpec((9 * K, K), lambda i: (0, 0)),
            pl.BlockSpec((XROWS, K), lambda i: (i, 0)),
        ],
        out_specs=pl.BlockSpec((XROWS, K), lambda i: (i, 0)),
        scratch_shapes=[pltpu.VMEM((9 * K, K), F32)],
        compiler_params=pltpu.CompilerParams(vmem_limit_bytes=32 * 1024 * 1024),
        name="blend",
    )(blend, following)
    return out.reshape(ensemble.shape)


def solution(mesh):
    placed = (
        P("gx", "gy", None, None),
        P("gx", "gy", None),
        P("gx", "gy", None),
        P("gx", "gy", None),
        P(),
    )
    return jax.shard_map(
        shards, mesh=mesh, in_specs=placed, out_specs=P("gx", "gy", None, None), check_vma=False
    )
```

profile of v0, /device:TPU:1, one launch (start us, length us, event | category | flops | bytes accessed | tf_op | source)
XLA Modules:
  0.0 79.2 jit_solution(15843800875409704771)
XLA Ops:
  0.0 0.0 copy-start
  0.0 2.8 %copy-done = bf16[16,32,48,128]{3,2,1,0:T(8,128)(2,1)S(1)} copy-done((bf16[16,32,48,128]{3,2,1,0:T(8,128)(2,1)S(1)}, bf16[16,32,48,128]{3,2,1,0:T(8,128)(2,1)}, u32[]{:S(2)}) %copy-start) | copy-done | bytes 6291480
  2.8 0.0 copy-start.1
  2.8 0.7 copy-done.1
  3.5 0.0 copy-start.2
  3.5 0.7 copy-done.2
  4.2 0.0 copy-start.3
  4.2 0.7 copy-done.3
  4.9 0.0 copy-start.4
  4.9 0.7 copy-done.4
  5.6 62.7 %analyse.1 = (bf16[24576,128]{1,0:T(8,128)(2,1)S(1)}, bf16[1152,128]{1,0:T(8,128)(2,1)S(1)}) custom-call(s32[8,16]{1,0:T(8,128)S(1)} %copy-done.4, s32[1,2048]{1,0:T(1,128)S(1)} %bitcast.6, s32[1,2048]{1,0:T(1,128)S(1)} %bitcast.7, f32[1,2048]{1,0:T(1,128)S(1)} %bitcast.8, f32[1,2048]{1,0:T(1,128)S(1)} %bitcast.9, bf16[24576,128]{1,0:T(8,128)(2,1)S(1)} %bitcast.5), custom_call_target="tpu_custom_call" | custom-call | tf_op jit(solution)/shard_map/analyse/pallas_call | solution.py:350
  68.3 10.9 %blend.1 = bf16[24576,128]{1,0:T(8,128)(2,1)} custom-call(bf16[1152,128]{1,0:T(8,128)(2,1)S(1)} %get-tuple-element.7.blend_ref, bf16[24576,128]{1,0:T(8,128)(2,1)S(1)} %get-tuple-element.8.ens_ref), custom_call_target="tpu_custom_call" | custom-call | tf_op jit(solution)/shard_map/blend/pallas_call | solution.py:384
Async XLA Ops:
  0.0 2.8 %copy-start = (bf16[16,32,48,128]{3,2,1,0:T(8,128)(2,1)S(1)}, bf16[16,32,48,128]{3,2,1,0:T(8,128)(2,1)}, u32[]{:S(2)}) copy-start(bf16[16,32,48,128]{3,2,1,0:T(8,128)(2,1)} %param.5) | copy-start | bytes 18874372
  2.8 0.7 copy-start.1
  3.5 0.7 copy-start.2
  4.2 0.7 copy-start.3
  4.9 0.7 copy-start.4
where the time goes:
time: 79.5 us; the launch traced here: 79.2 us
  Pallas kernels  73.6 us (93%)
  local copies, waits for them, and re-layouts  5.56 us (7%)
    pallas_call x1, Pallas kernels, shards(): pl.pallas_call(first_kernel, out_shape=(jax.ShapeDtypeStruct((ROWS, K), B...  62.7 us
    pallas_call x1, Pallas kernels, shards(): pl.pallas_call(last_kernel, grid=(CX,), out_shape=jax.ShapeDtypeStruct((R...  10.9 us
    unnamed x10, local copies, waits for them, and re-layouts  5.56 us

commit v1 on v0

--- a/solution.py
+++ b/solution.py
@@ -16,14 +16,16 @@
 ITERS = 2
 PACK = 72
 QUART = 256
-GROUP = 4
+GROUP = 8
+BX = 8
+BY = 16
 
 MESH = pl.DeviceIdType.MESH
 F32 = jnp.float32
 BF16 = jnp.bfloat16
-STAT_STEPS = (-2, -1, 1, 2)
-STAT_WEIGHTS = (0.5, 0.75, 0.75, 0.5)
-BLEND_STEPS = tuple((a, b) for a in (-1, 0, 1) for b in (-1, 0, 1) if (a, b) != (0, 0))
+STAT_STEPS = (-1, 1, -2, 2)
+STAT_WEIGHTS = (0.75, 0.75, 0.5, 0.5)
+BLEND_STEPS = tuple((a, b) for a in (-1, 1, 0) for b in (-1, 1, 0) if (a, b) != (0, 0))
 
 
 def slot_of(a, b):
@@ -126,45 +128,81 @@
     return below, 1.0 - below - above, above
 
 
-def apply_column(i, matrix_ref, read, write):
-    position = (i.astype(F32) + 0.5) / CX
-    weights = hats(position)
-    sides = []
+def blend_column(i, slot, matrices, stationary):
+    weights = hats((i.astype(F32) + 0.5) / CX)
     for b in range(3):
-        blend = weights[0] * matrix_ref[b * K : (b + 1) * K]
+        blend = weights[0] * matrices[b * K : (b + 1) * K]
         for a in (1, 2):
             at = (a * 3 + b) * K
-            blend = blend + weights[a] * matrix_ref[at : at + K]
-        sides.append(wide(blend))
+            blend = blend + weights[a] * matrices[at : at + K]
+        stationary[slot, b * K : (b + 1) * K] = wide(blend)
+
+
+def apply_column(i, slot, ens, stationary):
     for half in range(2):
-        stationary = jnp.concatenate([sides[half], sides[half + 1]], axis=0)
+        matrix = stationary[slot, half * K : half * K + 2 * K]
         for group in range(CY // 2 // GROUP):
             first = half * (CY // 2) + group * GROUP
-            block = read(first * LEV, GROUP * LEV)
-            out = mm_nt(jnp.concatenate([block, block], axis=1), stationary)
+            here = pl.ds(pl.multiple_of(i * XROWS + first * LEV, 16), GROUP * LEV)
+            block = ens[here]
+            out = mm_nt(jnp.concatenate([block, block], axis=1), matrix)
             parts = []
             for j in range(GROUP):
                 hat = hat_of(first + j, CY)
                 piece = out[j * LEV : (j + 1) * LEV]
                 parts.append(hat[half] * piece[:, :K] + hat[half + 1] * piece[:, K:])
-            write(first * LEV, GROUP * LEV, jnp.concatenate(parts, axis=0).astype(BF16))
+            ens[here] = jnp.concatenate(parts, axis=0).astype(BF16)
+
+
+def apply_columns(first, last, matrices, stationary, ens, before, after):
+    blend_column(jnp.int32(first), 0, matrices, stationary)
+
+    @pl.loop(first // 2, last // 2)
+    def _(pair):
+        for slot in range(2):
+            before(pair * 2 + slot)
+        for slot in range(2):
+            i = pair * 2 + slot
+            apply_column(i, slot, ens, stationary)
+            blend_column(jnp.minimum(i + 1, CX - 1), 1 - slot, matrices, stationary)
+        for slot in range(2):
+            after(pair * 2 + slot)
 
 
 def full_matrices(transforms):
     return mm(transforms, centring()) + 1.0 / K
 
 
+def column(ref, i):
+    return ref.at[pl.ds(pl.multiple_of(i * XROWS, XROWS), XROWS)]
+
+
 def first_kernel(
-    count_ref, cell_ref, cells_ref, value_ref, weight_ref, ens_ref,
+    count_any, cell_any, value_any, weight_any, ens_any,
     next_ref, blend_ref,
-    ens, ens32, picked, rows, matrices, matrices2, stat_x, stat_y, got_x, got_y, nearby,
-    load_sem, store_sem, send_x, recv_x, send_y, recv_y, send_t, recv_t,
+    count_ref, cell_ref, given, cells_ref, ens, ens32, picked, rows, matrices, matrices2, stationary,
+    stat_x, stat_y, got_x, got_y, nearby, own_ref,
+    small_sem, load_sem, store_sem, own_sem, send_x, recv_x, send_y, recv_y, send_t, recv_t,
 ):
     gx, gy = lax.axis_index("gx"), lax.axis_index("gy")
     nx, ny = lax.axis_size("gx"), lax.axis_size("gy")
 
     def at(a, b):
         return (lax.rem(gx + a + nx, nx), lax.rem(gy + b + ny, ny))
+
+    small = [
+        pltpu.make_async_copy(count_any, count_ref, small_sem.at[0]),
+        pltpu.make_async_copy(cell_any, cell_ref, small_sem.at[1]),
+        pltpu.make_async_copy(cell_any, cells_ref, small_sem.at[2]),
+        pltpu.make_async_copy(value_any, given.at[0], small_sem.at[3]),
+        pltpu.make_async_copy(weight_any, given.at[1], small_sem.at[4]),
+    ]
+    for copy in small:
+        copy.start()
+
+    @pl.loop(0, CX)
+    def _(i):
+        pltpu.make_async_copy(column(ens_any, i), column(ens, i), load_sem.at[i]).start()
 
     partners = [(s, 0) for s in STAT_STEPS] + [(0, s) for s in STAT_STEPS]
     partners += [(a, b) for a in (-1, 1) for b in (-1, 1)]
@@ -172,18 +210,13 @@
     for a, b in partners:
         pl.semaphore_signal(barrier, inc=1, device_id=at(a, b), device_id_type=MESH)
 
-    def column(ref, i):
-        return ref.at[pl.ds(pl.multiple_of(i * XROWS, XROWS), XROWS)]
-
-    @pl.loop(0, CX)
-    def _(i):
-        pltpu.make_async_copy(column(ens_ref, i), column(ens, i), load_sem.at[i]).start()
-
+    for copy in small:
+        copy.wait()
     count = count_ref[gx, gy]
     cells = cells_ref[...].astype(F32)
     slot = lax.broadcasted_iota(jnp.int32, (1, OBS), 1)
-    rows[0:1] = jnp.where(slot < count, weight_ref[...], 0.0)
-    rows[1:2] = value_ref[...]
+    rows[0:1] = jnp.where(slot < count, given[1], 0.0)
+    rows[1:2] = given[0]
     east = jnp.floor((cells + 0.5) * (1.0 / XROWS))
     north = jnp.floor((cells - XROWS * east + 0.5) * (1.0 / LEV))
     for first, hat in ((2, hats((east + 0.5) / CX)), (5, hats((north + 0.5) / CY))):
@@ -192,7 +225,7 @@
 
     @pl.loop(0, CX)
     def _(i):
-        pltpu.make_async_copy(column(ens_ref, i), column(ens, i), load_sem.at[i]).wait()
+        pltpu.make_async_copy(column(ens_any, i), column(ens, i), load_sem.at[i]).wait()
         start = pl.multiple_of(i * XROWS, XROWS)
         ens32[pl.ds(start, XROWS)] = ens[pl.ds(start, XROWS)].astype(F32)
 
@@ -237,19 +270,14 @@
             total = total + STAT_WEIGHTS[k] * got[t, k]
         return total
 
+    def nothing(i):
+        pass
+
+    def store(i):
+        pltpu.make_async_copy(column(ens, i), column(next_ref, i), store_sem.at[i]).start()
+
     def apply_some(first, last):
-        @pl.loop(first, last)
-        def _(i):
-            base = i * XROWS
-
-            def read(start, size):
-                return ens[pl.ds(pl.multiple_of(base + start, 16), size)]
-
-            def write(start, size, value):
-                ens[pl.ds(pl.multiple_of(base + start, 16), size)] = value
-
-            apply_column(i, matrices, read, write)
-            pltpu.make_async_copy(column(ens, i), column(next_ref, i), store_sem.at[i]).start()
+        apply_columns(first, last, matrices, stationary, ens, nothing, store)
 
     for t in range(ITERS):
         total = jnp.zeros((K + 16, K), F32)
@@ -285,24 +313,24 @@
         for copy in copies:
             copy.start()
         if t == 1:
-            apply_some(0, 5)
+            apply_some(0, CX // 2)
         finish(copies)
         stat_y[t] = weighted(t, stat_x, got_x)
         copies = exchange(t, stat_y, got_y, send_y, recv_y, lambda step: (0, step))
         for copy in copies:
             copy.start()
         if t == 1:
-            apply_some(5, 10)
+            apply_some(CX // 2, CX)
         finish(copies)
-        own = slot_of(0, 0) * K
-        nearby[t, own : own + K] = transposed_transform(weighted(t, stat_y, got_y))
+        own_ref[t] = transposed_transform(weighted(t, stat_y, got_y))
+        landing = nearby if t == 0 else blend_ref
         copies = []
         for k, (a, b) in enumerate(BLEND_STEPS):
             there = slot_of(-a, -b)
             copies.append(
                 pltpu.make_async_remote_copy(
-                    src_ref=nearby.at[t, pl.ds(own, K)],
-                    dst_ref=nearby.at[t, pl.ds(there * K, K)],
+                    src_ref=own_ref.at[t],
+                    dst_ref=landing.at[pl.ds(there * K, K)],
                     send_sem=send_t.at[t, k],
                     recv_sem=recv_t.at[t, there],
                     device_id=at(a, b),
@@ -311,40 +339,45 @@
             )
         for copy in copies:
             copy.start()
-        if t == 1:
-            apply_some(10, 16)
+        own = slot_of(0, 0) * K
+        mine = pltpu.make_async_copy(own_ref.at[t], landing.at[pl.ds(own, K)], own_sem.at[t])
+        mine.start()
         finish(copies)
+        mine.wait()
         if t == 0:
-            matrices[...] = full_matrices(nearby[t])
-
-    blend_ref[...] = nearby[1]
+            matrices[...] = full_matrices(nearby[...])
 
     @pl.loop(0, CX)
     def _(i):
         pltpu.make_async_copy(column(ens, i), column(next_ref, i), store_sem.at[i]).wait()
 
 
-def last_kernel(blend_ref, ens_ref, out_ref, matrices):
-    i = pl.program_id(0)
-
-    @pl.when(i == 0)
-    def _():
-        matrices[...] = full_matrices(blend_ref[...])
-
-    def read(start, size):
-        return ens_ref[start : start + size]
-
-    def write(start, size, value):
-        out_ref[start : start + size] = value
-
-    apply_column(i, matrices, read, write)
+def last_kernel(blend_any, ens_any, out_any, nearby, ens, matrices, stationary, blend_sem, load_sem, store_sem):
+    get = pltpu.make_async_copy(blend_any, nearby, blend_sem)
+    get.start()
+
+    @pl.loop(0, CX)
+    def _(i):
+        pltpu.make_async_copy(column(ens_any, i), column(ens, i), load_sem.at[i]).start()
+
+    get.wait()
+    matrices[...] = full_matrices(nearby[...])
+
+    def load(i):
+        pltpu.make_async_copy(column(ens_any, i), column(ens, i), load_sem.at[i]).wait()
+
+    def store(i):
+        pltpu.make_async_copy(column(ens, i), column(out_any, i), store_sem.at[i]).start()
+
+    apply_columns(0, CX, matrices, stationary, ens, load, store)
+
+    @pl.loop(0, CX)
+    def _(i):
+        pltpu.make_async_copy(column(ens, i), column(out_any, i), store_sem.at[i]).wait()
 
 
 def shards(ensemble, obs_cell, obs_value, obs_weight, obs_count):
     flat = ensemble.reshape(ROWS, K)
-    cells = obs_cell.reshape(1, OBS)
-    vmem = pl.BlockSpec(memory_space=pltpu.VMEM)
-    smem = pl.BlockSpec(memory_space=pltpu.SMEM)
     anywhere = pl.BlockSpec(memory_space=pl.ANY)
     dma = pltpu.SemaphoreType.DMA
     following, blend = pl.pallas_call(
@@ -353,22 +386,30 @@
             jax.ShapeDtypeStruct((ROWS, K), BF16),
             jax.ShapeDtypeStruct((9 * K, K), BF16),
         ),
-        in_specs=[smem, smem, vmem, vmem, vmem, anywhere],
-        out_specs=(anywhere, vmem),
+        in_specs=[anywhere] * 5,
+        out_specs=(anywhere, anywhere),
         scratch_shapes=[
+            pltpu.SMEM((BX, BY), jnp.int32),
+            pltpu.SMEM((1, OBS), jnp.int32),
+            pltpu.VMEM((2, 1, OBS), F32),
+            pltpu.VMEM((1, OBS), jnp.int32),
             pltpu.VMEM((ROWS, K), BF16),
             pltpu.VMEM((ROWS, K), F32),
             pltpu.VMEM((OBS, K), F32),
             pltpu.VMEM((8, OBS), F32),
             pltpu.VMEM((9 * K, K), F32),
             pltpu.VMEM((9 * K, 2 * K), BF16),
+            pltpu.VMEM((2, 3 * K, 2 * K), BF16),
             pltpu.VMEM((ITERS, PACK, K), F32),
             pltpu.VMEM((ITERS, PACK, K), F32),
             pltpu.VMEM((ITERS, 4, PACK, K), F32),
             pltpu.VMEM((ITERS, 4, PACK, K), F32),
-            pltpu.VMEM((ITERS, 9 * K, K), BF16),
+            pltpu.VMEM((9 * K, K), BF16),
+            pltpu.VMEM((ITERS, K, K), BF16),
+            dma((5,)),
             dma((CX,)),
             dma((CX,)),
+            dma((ITERS,)),
             dma((ITERS, 4)),
             dma((ITERS, 4)),
             dma((ITERS, 4)),
@@ -377,21 +418,31 @@
             dma((ITERS, 9)),
         ],
         compiler_params=pltpu.CompilerParams(
-            collective_id=0, has_side_effects=True, vmem_limit_bytes=40 * 1024 * 1024
+            collective_id=0, has_side_effects=True, vmem_limit_bytes=58 * 1024 * 1024
         ),
         name="analyse",
-    )(obs_count, cells, cells, obs_value.reshape(1, OBS), obs_weight.reshape(1, OBS), flat)
+    )(
+        obs_count,
+        obs_cell.reshape(1, OBS),
+        obs_value.reshape(1, OBS),
+        obs_weight.reshape(1, OBS),
+        flat,
+    )
     out = pl.pallas_call(
         last_kernel,
-        grid=(CX,),
         out_shape=jax.ShapeDtypeStruct((ROWS, K), BF16),
-        in_specs=[
-            pl.BlockSpec((9 * K, K), lambda i: (0, 0)),
-            pl.BlockSpec((XROWS, K), lambda i: (i, 0)),
+        in_specs=[anywhere] * 2,
+        out_specs=anywhere,
+        scratch_shapes=[
+            pltpu.VMEM((9 * K, K), BF16),
+            pltpu.VMEM((ROWS, K), BF16),
+            pltpu.VMEM((9 * K, K), F32),
+            pltpu.VMEM((2, 3 * K, 2 * K), BF16),
+            dma(()),
+            dma((CX,)),
+            dma((CX,)),
         ],
-        out_specs=pl.BlockSpec((XROWS, K), lambda i: (i, 0)),
-        scratch_shapes=[pltpu.VMEM((9 * K, K), F32)],
-        compiler_params=pltpu.CompilerParams(vmem_limit_bytes=32 * 1024 * 1024),
+        compiler_params=pltpu.CompilerParams(vmem_limit_bytes=58 * 1024 * 1024),
         name="blend",
     )(blend, following)
     return out.reshape(ensemble.shape)

time: 79.5 us -> 73.1 us (0.919)
  local copies, waits for them, and re-layouts: 5.56 us -> 0 us
  Pallas kernels: 73.6 us -> 72.3 us
    pallas_call x1, Pallas kernels: 62.7 us -> 55.3 us  [shards(): pl.pallas_call(first_kernel, out_shape=(jax.ShapeDtypeStruct((ROWS, K), B...]
    pallas_call x1, Pallas kernels: 10.9 us -> 17 us  [shards(): pl.pallas_call(last_kernel, out_shape=jax.ShapeDtypeStruct((ROWS, K), BF1...]
    unnamed x10 -> x0, local copies, waits for them, and re-layouts: 5.56 us -> none
where the time goes in v1:
time: 73.1 us; the launch traced here: 72.4 us
  Pallas kernels  72.3 us (99%)
    pallas_call x1, Pallas kernels, shards(): pl.pallas_call(first_kernel, out_shape=(jax.ShapeDtypeStruct((ROWS, K), B...  55.3 us
    pallas_call x1, Pallas kernels, shards(): pl.pallas_call(last_kernel, out_shape=jax.ShapeDtypeStruct((ROWS, K), BF1...  17 us

profile of v1, /device:TPU:1, one launch (start us, length us, event | category | flops | bytes accessed | tf_op | source)
XLA Modules:
  0.0 72.4 jit_solution(10649904858699507164)
XLA Ops:
  0.0 55.3 %analyse.1 = (bf16[24576,128]{1,0:T(8,128)(2,1)}, bf16[1152,128]{1,0:T(8,128)(2,1)}) custom-call(s32[8,16]{1,0:T(8,128)} %count_any.1, s32[1,2048]{1,0:T(1,128)} %bitcast.6, f32[1,2048]{1,0:T(1,128)} %bitcast.7, f32[1,2048]{1,0:T(1,128)} %bitcast.8, bf16[24576,128]{1,0:T(8,128)(2,1)} %bitcast.5), custom_call_target="tpu_custom_call" | custom-call | tf_op jit(solution)/shard_map/analyse/pallas_call | solution.py:383
  55.4 17.0 %blend.1 = bf16[24576,128]{1,0:T(8,128)(2,1)} custom-call(bf16[1152,128]{1,0:T(8,128)(2,1)} %get-tuple-element.7.blend_any, bf16[24576,128]{1,0:T(8,128)(2,1)} %get-tuple-element.8.ens_any), custom_call_target="tpu_custom_call" | custom-call | tf_op jit(solution)/shard_map/blend/pallas_call | solution.py:431

commit v2 on v1

--- a/solution.py
+++ b/solution.py
@@ -138,7 +138,7 @@
         stationary[slot, b * K : (b + 1) * K] = wide(blend)
 
 
-def apply_column(i, slot, ens, stationary):
+def apply_column(i, slot, ens, fresh, stationary):
     for half in range(2):
         matrix = stationary[slot, half * K : half * K + 2 * K]
         for group in range(CY // 2 // GROUP):
@@ -151,10 +151,10 @@
                 hat = hat_of(first + j, CY)
                 piece = out[j * LEV : (j + 1) * LEV]
                 parts.append(hat[half] * piece[:, :K] + hat[half + 1] * piece[:, K:])
-            ens[here] = jnp.concatenate(parts, axis=0).astype(BF16)
-
-
-def apply_columns(first, last, matrices, stationary, ens, before, after):
+            fresh[here] = jnp.concatenate(parts, axis=0).astype(BF16)
+
+
+def apply_columns(first, last, matrices, stationary, ens, fresh, before, after):
     blend_column(jnp.int32(first), 0, matrices, stationary)
 
     @pl.loop(first // 2, last // 2)
@@ -163,7 +163,7 @@
             before(pair * 2 + slot)
         for slot in range(2):
             i = pair * 2 + slot
-            apply_column(i, slot, ens, stationary)
+            apply_column(i, slot, ens, fresh, stationary)
             blend_column(jnp.minimum(i + 1, CX - 1), 1 - slot, matrices, stationary)
         for slot in range(2):
             after(pair * 2 + slot)
@@ -180,7 +180,7 @@
 def first_kernel(
     count_any, cell_any, value_any, weight_any, ens_any,
     next_ref, blend_ref,
-    count_ref, cell_ref, given, cells_ref, ens, ens32, picked, rows, matrices, matrices2, stationary,
+    count_ref, cell_ref, given, cells_ref, ens, applied, ens32, picked, rows, matrices, matrices2, stationary,
     stat_x, stat_y, got_x, got_y, nearby, own_ref,
     small_sem, load_sem, store_sem, own_sem, send_x, recv_x, send_y, recv_y, send_t, recv_t,
 ):
@@ -274,10 +274,10 @@
         pass
 
     def store(i):
-        pltpu.make_async_copy(column(ens, i), column(next_ref, i), store_sem.at[i]).start()
+        pltpu.make_async_copy(column(applied, i), column(next_ref, i), store_sem.at[i]).start()
 
     def apply_some(first, last):
-        apply_columns(first, last, matrices, stationary, ens, nothing, store)
+        apply_columns(first, last, matrices, stationary, ens, applied, nothing, store)
 
     for t in range(ITERS):
         total = jnp.zeros((K + 16, K), F32)
@@ -349,10 +349,10 @@
 
     @pl.loop(0, CX)
     def _(i):
-        pltpu.make_async_copy(column(ens, i), column(next_ref, i), store_sem.at[i]).wait()
-
-
-def last_kernel(blend_any, ens_any, out_any, nearby, ens, matrices, stationary, blend_sem, load_sem, store_sem):
+        pltpu.make_async_copy(column(applied, i), column(next_ref, i), store_sem.at[i]).wait()
+
+
+def last_kernel(blend_any, ens_any, out_any, nearby, ens, applied, matrices, stationary, blend_sem, load_sem, store_sem):
     get = pltpu.make_async_copy(blend_any, nearby, blend_sem)
     get.start()
 
@@ -367,13 +367,13 @@
         pltpu.make_async_copy(column(ens_any, i), column(ens, i), load_sem.at[i]).wait()
 
     def store(i):
-        pltpu.make_async_copy(column(ens, i), column(out_any, i), store_sem.at[i]).start()
-
-    apply_columns(0, CX, matrices, stationary, ens, load, store)
+        pltpu.make_async_copy(column(applied, i), column(out_any, i), store_sem.at[i]).start()
+
+    apply_columns(0, CX, matrices, stationary, ens, applied, load, store)
 
     @pl.loop(0, CX)
     def _(i):
-        pltpu.make_async_copy(column(ens, i), column(out_any, i), store_sem.at[i]).wait()
+        pltpu.make_async_copy(column(applied, i), column(out_any, i), store_sem.at[i]).wait()
 
 
 def shards(ensemble, obs_cell, obs_value, obs_weight, obs_count):
@@ -393,6 +393,7 @@
             pltpu.SMEM((1, OBS), jnp.int32),
             pltpu.VMEM((2, 1, OBS), F32),
             pltpu.VMEM((1, OBS), jnp.int32),
+            pltpu.VMEM((ROWS, K), BF16),
             pltpu.VMEM((ROWS, K), BF16),
             pltpu.VMEM((ROWS, K), F32),
             pltpu.VMEM((OBS, K), F32),
@@ -436,6 +437,7 @@
         scratch_shapes=[
             pltpu.VMEM((9 * K, K), BF16),
             pltpu.VMEM((ROWS, K), BF16),
+            pltpu.VMEM((ROWS, K), BF16),
             pltpu.VMEM((9 * K, K), F32),
             pltpu.VMEM((2, 3 * K, 2 * K), BF16),
             dma(()),

time: 73.1 us -> 57.4 us (0.79)
  Pallas kernels: 72.3 us -> 57.3 us
    pallas_call x1, Pallas kernels: 17 us -> 7.43 us  [shards(): pl.pallas_call(last_kernel, out_shape=jax.ShapeDtypeStruct((ROWS, K), BF1...]
    pallas_call x1, Pallas kernels: 55.3 us -> 49.9 us  [shards(): pl.pallas_call(first_kernel, out_shape=(jax.ShapeDtypeStruct((ROWS, K), B...]
where the time goes in v2:
time: 57.4 us; the launch traced here: 57.3 us
  Pallas kernels  57.3 us (100%)
    pallas_call x1, Pallas kernels, shards(): pl.pallas_call(first_kernel, out_shape=(jax.ShapeDtypeStruct((ROWS, K), B...  49.9 us
    pallas_call x1, Pallas kernels, shards(): pl.pallas_call(last_kernel, out_shape=jax.ShapeDtypeStruct((ROWS, K), BF1...  7.43 us

profile of v2, /device:TPU:1, one launch (start us, length us, event | category | flops | bytes accessed | tf_op | source)
XLA Modules:
  0.0 57.3 jit_solution(18285679862448693258)
XLA Ops:
  0.0 49.9 %analyse.1 = (bf16[24576,128]{1,0:T(8,128)(2,1)}, bf16[1152,128]{1,0:T(8,128)(2,1)}) custom-call(s32[8,16]{1,0:T(8,128)} %count_any.1, s32[1,2048]{1,0:T(1,128)} %bitcast.6, f32[1,2048]{1,0:T(1,128)} %bitcast.7, f32[1,2048]{1,0:T(1,128)} %bitcast.8, bf16[24576,128]{1,0:T(8,128)(2,1)} %bitcast.5), custom_call_target="tpu_custom_call" | custom-call | tf_op jit(solution)/shard_map/analyse/pallas_call | solution.py:383
  49.9 7.4 %blend.1 = bf16[24576,128]{1,0:T(8,128)(2,1)} custom-call(bf16[1152,128]{1,0:T(8,128)(2,1)} %get-tuple-element.7.blend_any, bf16[24576,128]{1,0:T(8,128)(2,1)} %get-tuple-element.8.ens_any), custom_call_target="tpu_custom_call" | custom-call | tf_op jit(solution)/shard_map/blend/pallas_call | solution.py:432

commit v3 on v2

--- a/solution.py
+++ b/solution.py
@@ -17,6 +17,9 @@
 PACK = 72
 QUART = 256
 GROUP = 8
+UNROLL = 4
+GATHER = 64
+PACKED = 80
 BX = 8
 BY = 16
 
@@ -66,33 +69,59 @@
     return jnp.where(row == col, (K - 1.0) / K, -1.0 / K).astype(BF16)
 
 
-def pack_stats(total):
+def fold(matrix):
     half = K // 2
     row, lane = iotas((half, K))
-    top = total[:half]
-    turned = pltpu.roll(total[half:K], half, 1)
-    body = jnp.where(lane < row, turned, top)
-    diagonal = jnp.sum(jnp.where(lane == row, turned, 0.0), axis=0, keepdims=True)
-    tail_row, _ = iotas((8, K))
-    projected = total[K : K + 1]
-    tail = jnp.where(tail_row == 0, diagonal, projected)
-    return jnp.concatenate([body, tail], axis=0)
+    return jnp.where(lane < row, pltpu.roll(matrix[half:], half, 1), matrix[:half])
+
+
+def unfold(body, diagonal):
+    half = K // 2
+    row, lane = iotas((half, K))
+    flipped = jnp.concatenate([body, jnp.zeros((half, K), F32)], axis=0).T
+    top = jnp.where(lane < row, flipped[:half], body)
+    lower = jnp.where(lane < row, body, flipped[:half])
+    bottom = jnp.where(lane < half, flipped[half:], pltpu.roll(lower, half, 1))
+    row, col = iotas((K, K))
+    return jnp.where(row == col, diagonal, jnp.concatenate([top, bottom], axis=0))
+
+
+def diagonal_of(matrix):
+    row, col = iotas((K, K))
+    return jnp.sum(jnp.where(row == col, matrix, 0.0), axis=0, keepdims=True)
+
+
+def pack_stats(total):
+    gram = total[:K]
+    tail_row, _ = iotas((PACK - K // 2, K))
+    tail = jnp.where(tail_row == 0, diagonal_of(gram), total[K : K + 1])
+    return jnp.concatenate([fold(gram), tail], axis=0)
 
 
 def unpack_stats(packed):
     half = K // 2
-    row, lane = iotas((half, K))
-    body = packed[:half]
-    diagonal = packed[half : half + 1]
-    projected = packed[half + 1 : half + 2]
-    flipped = jnp.concatenate([body, jnp.zeros((half, K), F32)], axis=0).T
-    top = jnp.where(lane < row, flipped[:half], body)
-    lower = jnp.where(lane < row, body, jnp.where(lane == row, diagonal, flipped[:half]))
-    bottom = jnp.where(lane < half, flipped[half:], pltpu.roll(lower, half, 1))
-    return jnp.concatenate([top, bottom], axis=0), projected
-
-
-def transposed_transform(packed):
+    return unfold(packed[:half], packed[half : half + 1]), packed[half + 1 : half + 2]
+
+
+def pack_transform(spread, weights):
+    tail_row, _ = iotas((PACKED - K // 2, K))
+    tail = jnp.zeros((PACKED - K // 2, K), F32)
+    for k, line in enumerate((diagonal_of(spread), weights)):
+        high, low = split(line)
+        tail = jnp.where(tail_row == 2 * k, high.astype(F32), tail)
+        tail = jnp.where(tail_row == 2 * k + 1, low.astype(F32), tail)
+    return jnp.concatenate([fold(spread), tail], axis=0).astype(BF16)
+
+
+def unpack_transform(packed):
+    half = K // 2
+    packed = packed.astype(F32)
+    diagonal = packed[half : half + 1] + packed[half + 1 : half + 2]
+    weights = packed[half + 2 : half + 3] + packed[half + 3 : half + 4]
+    return (weights + unfold(packed[:half], diagonal)).astype(BF16)
+
+
+def transform_parts(packed):
     gram, projected = unpack_stats(packed)
     row, col = iotas((K, K))
     identity = jnp.where(row == col, 1.0, 0.0).astype(F32)
@@ -102,18 +131,15 @@
     root = system / frobenius
     carried = jnp.broadcast_to(projected, (16, K))
     correction = 1.5 * identity - 0.5 * root
-    out = times(jnp.concatenate([root, carried], axis=0), correction)
-    root, carried, inverse = out[:K], out[K:], correction
+    root, carried, inverse = times(root, correction), times(carried, correction), correction
     for step in range(1, NEWTON):
         correction = 1.5 * identity - 0.5 * times(inverse, root)
+        out = times(jnp.concatenate([inverse, carried], axis=0), correction)
         if step < NEWTON - 1:
-            out = times(jnp.concatenate([inverse, carried, root], axis=0), correction)
-            root = out[K + 16 :]
-        else:
-            out = times(jnp.concatenate([inverse, carried], axis=0), correction)
-        inverse, carried = out[:K], out[K : K + 16]
+            root = times(root, correction)
+        inverse, carried = out[:K], out[K:]
     weights = times(carried, inverse)[0:1] / frobenius
-    return (weights + jnp.sqrt((K - 1) / frobenius) * inverse).astype(BF16)
+    return jnp.sqrt((K - 1) / frobenius) * inverse, weights
 
 
 def hats(position):
@@ -157,16 +183,16 @@
 def apply_columns(first, last, matrices, stationary, ens, fresh, before, after):
     blend_column(jnp.int32(first), 0, matrices, stationary)
 
-    @pl.loop(first // 2, last // 2)
-    def _(pair):
-        for slot in range(2):
-            before(pair * 2 + slot)
-        for slot in range(2):
-            i = pair * 2 + slot
-            apply_column(i, slot, ens, fresh, stationary)
-            blend_column(jnp.minimum(i + 1, CX - 1), 1 - slot, matrices, stationary)
-        for slot in range(2):
-            after(pair * 2 + slot)
+    @pl.loop(first // UNROLL, last // UNROLL)
+    def _(step):
+        for k in range(UNROLL):
+            before(step * UNROLL + k)
+        for k in range(UNROLL):
+            i = step * UNROLL + k
+            apply_column(i, k % 2, ens, fresh, stationary)
+            blend_column(jnp.minimum(i + 1, CX - 1), 1 - k % 2, matrices, stationary)
+        for k in range(UNROLL):
+            after(step * UNROLL + k)
 
 
 def full_matrices(transforms):
@@ -180,8 +206,8 @@
 def first_kernel(
     count_any, cell_any, value_any, weight_any, ens_any,
     next_ref, blend_ref,
-    count_ref, cell_ref, given, cells_ref, ens, applied, ens32, picked, rows, matrices, matrices2, stationary,
-    stat_x, stat_y, got_x, got_y, nearby, own_ref,
+    count_ref, cell_ref, given, cells_ref, ens, applied, ens32, picked, rows, deviations, matrices, stationary,
+    stat_x, stat_y, got_x, got_y, nearby, transforms, own_ref,
     small_sem, load_sem, store_sem, own_sem, send_x, recv_x, send_y, recv_y, send_t, recv_t,
 ):
     gx, gy = lax.axis_index("gx"), lax.axis_index("gy")
@@ -229,14 +255,13 @@
         start = pl.multiple_of(i * XROWS, XROWS)
         ens32[pl.ds(start, XROWS)] = ens[pl.ds(start, XROWS)].astype(F32)
 
-    @pl.loop(0, OBS // 16)
+    @pl.loop(0, OBS // GATHER)
     def _(g):
-        for r in range(16):
-            o = g * 16 + r
+        for r in range(GATHER):
+            o = g * GATHER + r
             picked[pl.ds(o, 1)] = ens32[pl.ds(cell_ref[0, o], 1)]
 
-    def accumulate(total, q, deviation, centre):
-        lanes = slice(q * QUART, (q + 1) * QUART)
+    def accumulate(total, lanes, deviation, centre):
         scale, value = rows[0:1, lanes], rows[1:2, lanes]
         anomaly = (scale * deviation).astype(BF16)
         innovation = jnp.broadcast_to(scale * (value - centre), (16, QUART)).astype(BF16)
@@ -286,25 +311,25 @@
             centre_rows = jnp.where(row == col, (K - 1.0) / K, jnp.where(row < K, -1.0 / K, 1.0 / K))
             centre_rows = centre_rows.astype(BF16)
             for q in range(OBS // QUART):
-                block = picked[q * QUART : (q + 1) * QUART].astype(BF16)
-                moved = mm_nt(centre_rows, block)
-                total = accumulate(total, q, moved[:K], moved[K : K + 1])
+                lanes = slice(q * QUART, (q + 1) * QUART)
+                moved = mm_nt(centre_rows, picked[lanes].astype(BF16))
+                total = accumulate(total, lanes, moved[:K], moved[K : K + 1])
+                deviations[:, lanes] = moved[:K].astype(BF16)
+                rows[8:9, lanes] = moved[K : K + 1]
         else:
-            matrices2[...] = wide(matrices[...])
             for q in range(OBS // QUART):
                 lanes = slice(q * QUART, (q + 1) * QUART)
-                block = picked[q * QUART : (q + 1) * QUART].astype(BF16)
-                block = jnp.concatenate([block, block], axis=1)
-                fresh = jnp.zeros((K, QUART), F32)
+                out = mm(transforms[...], deviations[:, lanes])
+                fresh = rows[8:9, lanes]
                 for a in range(3):
-                    out = mm_nt(matrices2[a * 3 * K : (a + 1) * 3 * K], block)
-                    part = rows[5:6, lanes] * out[:K]
-                    part = part + rows[6:7, lanes] * out[K : 2 * K]
-                    part = part + rows[7:8, lanes] * out[2 * K :]
+                    at_a = a * 3 * K
+                    part = rows[5:6, lanes] * out[at_a : at_a + K]
+                    part = part + rows[6:7, lanes] * out[at_a + K : at_a + 2 * K]
+                    part = part + rows[7:8, lanes] * out[at_a + 2 * K : at_a + 3 * K]
                     fresh = fresh + rows[2 + a : 3 + a, lanes] * part
                 fresh = fresh.astype(BF16).astype(F32)
                 centre = jnp.sum(fresh, axis=0, keepdims=True) * (1.0 / K)
-                total = accumulate(total, q, fresh - centre, centre)
+                total = accumulate(total, lanes, fresh - centre, centre)
         stat_x[t] = pack_stats(total)
 
         if t == 0:
@@ -313,6 +338,7 @@
         for copy in copies:
             copy.start()
         if t == 1:
+            matrices[...] = full_matrices(transforms[...])
             apply_some(0, CX // 2)
         finish(copies)
         stat_y[t] = weighted(t, stat_x, got_x)
@@ -322,37 +348,44 @@
         if t == 1:
             apply_some(CX // 2, CX)
         finish(copies)
-        own_ref[t] = transposed_transform(weighted(t, stat_y, got_y))
+        spread, weights = transform_parts(weighted(t, stat_y, got_y))
+        own_ref[t] = pack_transform(spread, weights)
         landing = nearby if t == 0 else blend_ref
-        copies = []
+        copies = {}
         for k, (a, b) in enumerate(BLEND_STEPS):
             there = slot_of(-a, -b)
-            copies.append(
-                pltpu.make_async_remote_copy(
-                    src_ref=own_ref.at[t],
-                    dst_ref=landing.at[pl.ds(there * K, K)],
-                    send_sem=send_t.at[t, k],
-                    recv_sem=recv_t.at[t, there],
-                    device_id=at(a, b),
-                    device_id_type=MESH,
-                )
+            copies[(-a, -b)] = pltpu.make_async_remote_copy(
+                src_ref=own_ref.at[t],
+                dst_ref=landing.at[there],
+                send_sem=send_t.at[t, k],
+                recv_sem=recv_t.at[t, there],
+                device_id=at(a, b),
+                device_id_type=MESH,
             )
-        for copy in copies:
+        for copy in copies.values():
             copy.start()
-        own = slot_of(0, 0) * K
-        mine = pltpu.make_async_copy(own_ref.at[t], landing.at[pl.ds(own, K)], own_sem.at[t])
-        mine.start()
-        finish(copies)
-        mine.wait()
+        own = slot_of(0, 0)
         if t == 0:
-            matrices[...] = full_matrices(nearby[...])
+            transforms[own * K : (own + 1) * K] = (weights + spread).astype(BF16)
+        else:
+            mine = pltpu.make_async_copy(own_ref.at[t], landing.at[own], own_sem)
+            mine.start()
+        for step in reversed(BLEND_STEPS):
+            copies[step].wait_recv()
+            if t == 0:
+                slot = slot_of(*step)
+                transforms[slot * K : (slot + 1) * K] = unpack_transform(nearby[slot])
+        if t == 1:
+            mine.wait()
+        for copy in copies.values():
+            copy.wait_send()
 
     @pl.loop(0, CX)
     def _(i):
         pltpu.make_async_copy(column(applied, i), column(next_ref, i), store_sem.at[i]).wait()
 
 
-def last_kernel(blend_any, ens_any, out_any, nearby, ens, applied, matrices, stationary, blend_sem, load_sem, store_sem):
+def last_kernel(blend_any, ens_any, out_any, nearby, ens, applied, transforms, matrices, stationary, blend_sem, load_sem, store_sem):
     get = pltpu.make_async_copy(blend_any, nearby, blend_sem)
     get.start()
 
@@ -361,7 +394,9 @@
         pltpu.make_async_copy(column(ens_any, i), column(ens, i), load_sem.at[i]).start()
 
     get.wait()
-    matrices[...] = full_matrices(nearby[...])
+    for slot in range(9):
+        transforms[slot * K : (slot + 1) * K] = unpack_transform(nearby[slot])
+    matrices[...] = full_matrices(transforms[...])
 
     def load(i):
         pltpu.make_async_copy(column(ens_any, i), column(ens, i), load_sem.at[i]).wait()
@@ -384,7 +419,7 @@
         first_kernel,
         out_shape=(
             jax.ShapeDtypeStruct((ROWS, K), BF16),
-            jax.ShapeDtypeStruct((9 * K, K), BF16),
+            jax.ShapeDtypeStruct((9, PACKED, K), BF16),
         ),
         in_specs=[anywhere] * 5,
         out_specs=(anywhere, anywhere),
@@ -397,20 +432,21 @@
             pltpu.VMEM((ROWS, K), BF16),
             pltpu.VMEM((ROWS, K), F32),
             pltpu.VMEM((OBS, K), F32),
-            pltpu.VMEM((8, OBS), F32),
+            pltpu.VMEM((16, OBS), F32),
+            pltpu.VMEM((K, OBS), BF16),
             pltpu.VMEM((9 * K, K), F32),
-            pltpu.VMEM((9 * K, 2 * K), BF16),
             pltpu.VMEM((2, 3 * K, 2 * K), BF16),
             pltpu.VMEM((ITERS, PACK, K), F32),
             pltpu.VMEM((ITERS, PACK, K), F32),
             pltpu.VMEM((ITERS, 4, PACK, K), F32),
             pltpu.VMEM((ITERS, 4, PACK, K), F32),
+            pltpu.VMEM((9, PACKED, K), BF16),
             pltpu.VMEM((9 * K, K), BF16),
-            pltpu.VMEM((ITERS, K, K), BF16),
+            pltpu.VMEM((ITERS, PACKED, K), BF16),
             dma((5,)),
             dma((CX,)),
             dma((CX,)),
-            dma((ITERS,)),
+            dma(()),
             dma((ITERS, 4)),
             dma((ITERS, 4)),
             dma((ITERS, 4)),
@@ -435,9 +471,10 @@
         in_specs=[anywhere] * 2,
         out_specs=anywhere,
         scratch_shapes=[
-            pltpu.VMEM((9 * K, K), BF16),
+            pltpu.VMEM((9, PACKED, K), BF16),
             pltpu.VMEM((ROWS, K), BF16),
             pltpu.VMEM((ROWS, K), BF16),
+            pltpu.VMEM((9 * K, K), BF16),
             pltpu.VMEM((9 * K, K), F32),
             pltpu.VMEM((2, 3 * K, 2 * K), BF16),
             dma(()),

time: 57.4 us -> 55.9 us (0.974)
  Pallas kernels: 57.3 us -> 55.8 us
    pallas_call x1, Pallas kernels: 49.9 us -> 48.7 us  [shards(): pl.pallas_call(first_kernel, out_shape=(jax.ShapeDtypeStruct((ROWS, K), B...]
where the time goes in v3:
time: 55.9 us; the launch traced here: 55.8 us
  Pallas kernels  55.8 us (100%)
    pallas_call x1, Pallas kernels, shards(): pl.pallas_call(first_kernel, out_shape=(jax.ShapeDtypeStruct((ROWS, K), B...  48.7 us
    pallas_call x1, Pallas kernels, shards(): pl.pallas_call(last_kernel, out_shape=jax.ShapeDtypeStruct((ROWS, K), BF1...  7.06 us

profile of v3, /device:TPU:1, one launch (start us, length us, event | category | flops | bytes accessed | tf_op | source)
XLA Modules:
  0.0 55.8 jit_solution(2240608802884885347)
XLA Ops:
  0.0 48.7 %analyse.1 = (bf16[24576,128]{1,0:T(8,128)(2,1)}, bf16[9,80,128]{2,1,0:T(8,128)(2,1)}) custom-call(s32[8,16]{1,0:T(8,128)} %count_any.1, s32[1,2048]{1,0:T(1,128)} %bitcast.6, f32[1,2048]{1,0:T(1,128)} %bitcast.7, f32[1,2048]{1,0:T(1,128)} %bitcast.8, bf16[24576,128]{1,0:T(8,128)(2,1)} %bitcast.5), custom_call_target="tpu_custom_call" | custom-call | tf_op jit(solution)/shard_map/analyse/pallas_call | solution.py:418
  48.8 7.1 %blend.1 = bf16[24576,128]{1,0:T(8,128)(2,1)} custom-call(bf16[9,80,128]{2,1,0:T(8,128)(2,1)} %get-tuple-element.7.blend_any, bf16[24576,128]{1,0:T(8,128)(2,1)} %get-tuple-element.8.ens_any), custom_call_target="tpu_custom_call" | custom-call | tf_op jit(solution)/shard_map/blend/pallas_call | solution.py:468

commit v4 on v3

--- a/solution.py
+++ b/solution.py
@@ -15,7 +15,7 @@
 NEWTON = 6
 ITERS = 2
 PACK = 72
-QUART = 256
+QUART = 512
 GROUP = 8
 UNROLL = 4
 GATHER = 64
@@ -129,15 +129,14 @@
     squares = jnp.sum(system * system, axis=0, keepdims=True)
     frobenius = jnp.sqrt(jnp.sum(squares, axis=1, keepdims=True))
     root = system / frobenius
-    carried = jnp.broadcast_to(projected, (16, K))
     correction = 1.5 * identity - 0.5 * root
-    root, carried, inverse = times(root, correction), times(carried, correction), correction
-    for step in range(1, NEWTON):
+    root, inverse = times(correction, root), correction
+    for step in range(1, NEWTON - 1):
         correction = 1.5 * identity - 0.5 * times(inverse, root)
-        out = times(jnp.concatenate([inverse, carried], axis=0), correction)
-        if step < NEWTON - 1:
-            root = times(root, correction)
-        inverse, carried = out[:K], out[K:]
+        root, inverse = times(correction, root), times(correction, inverse)
+    correction = 1.5 * identity - 0.5 * times(inverse, root)
+    carried = times(jnp.broadcast_to(projected, (16, K)), inverse)
+    carried, inverse = times(carried, correction), times(correction, inverse)
     weights = times(carried, inverse)[0:1] / frobenius
     return jnp.sqrt((K - 1) / frobenius) * inverse, weights
 
@@ -190,9 +189,8 @@
         for k in range(UNROLL):
             i = step * UNROLL + k
             apply_column(i, k % 2, ens, fresh, stationary)
+            after(i)
             blend_column(jnp.minimum(i + 1, CX - 1), 1 - k % 2, matrices, stationary)
-        for k in range(UNROLL):
-            after(step * UNROLL + k)
 
 
 def full_matrices(transforms):
@@ -283,16 +281,18 @@
             )
         return copies
 
-    def finish(copies):
-        for copy in copies:
-            copy.wait_recv()
-        for copy in copies:
-            copy.wait_send()
-
-    def weighted(t, sent, got):
+    pending = []
+
+    def settle():
+        while pending:
+            pending.pop().wait_send()
+
+    def weighted(t, sent, got, copies):
         total = sent[t]
-        for k in range(4):
+        for k in reversed(range(4)):
+            copies[STAT_STEPS.index(-STAT_STEPS[k])].wait_recv()
             total = total + STAT_WEIGHTS[k] * got[t, k]
+        pending.extend(copies)
         return total
 
     def nothing(i):
@@ -340,15 +340,14 @@
         if t == 1:
             matrices[...] = full_matrices(transforms[...])
             apply_some(0, CX // 2)
-        finish(copies)
-        stat_y[t] = weighted(t, stat_x, got_x)
+            settle()
+        stat_y[t] = weighted(t, stat_x, got_x, copies)
         copies = exchange(t, stat_y, got_y, send_y, recv_y, lambda step: (0, step))
         for copy in copies:
             copy.start()
         if t == 1:
             apply_some(CX // 2, CX)
-        finish(copies)
-        spread, weights = transform_parts(weighted(t, stat_y, got_y))
+        spread, weights = transform_parts(weighted(t, stat_y, got_y, copies))
         own_ref[t] = pack_transform(spread, weights)
         landing = nearby if t == 0 else blend_ref
         copies = {}
@@ -370,6 +369,7 @@
         else:
             mine = pltpu.make_async_copy(own_ref.at[t], landing.at[own], own_sem)
             mine.start()
+            settle()
         for step in reversed(BLEND_STEPS):
             copies[step].wait_recv()
             if t == 0:
@@ -377,8 +377,8 @@
                 transforms[slot * K : (slot + 1) * K] = unpack_transform(nearby[slot])
         if t == 1:
             mine.wait()
-        for copy in copies.values():
-            copy.wait_send()
+        pending.extend(copies.values())
+    settle()
 
     @pl.loop(0, CX)
     def _(i):

time: 55.9 us -> 54.5 us (0.975)
  Pallas kernels: 55.8 us -> 54.4 us
    pallas_call x1, Pallas kernels: 48.7 us -> 47.7 us  [shards(): pl.pallas_call(first_kernel, out_shape=(jax.ShapeDtypeStruct((ROWS, K), B...]
where the time goes in v4:
time: 54.5 us; the launch traced here: 54.4 us
  Pallas kernels  54.4 us (100%)
    pallas_call x1, Pallas kernels, shards(): pl.pallas_call(first_kernel, out_shape=(jax.ShapeDtypeStruct((ROWS, K), B...  47.7 us
    pallas_call x1, Pallas kernels, shards(): pl.pallas_call(last_kernel, out_shape=jax.ShapeDtypeStruct((ROWS, K), BF1...  6.71 us

profile of v4, /device:TPU:1, one launch (start us, length us, event | category | flops | bytes accessed | tf_op | source)
XLA Modules:
  0.0 54.4 jit_solution(6354323974922989031)
XLA Ops:
  0.0 47.7 %analyse.1 = (bf16[24576,128]{1,0:T(8,128)(2,1)}, bf16[9,80,128]{2,1,0:T(8,128)(2,1)}) custom-call(s32[8,16]{1,0:T(8,128)} %count_any.1, s32[1,2048]{1,0:T(1,128)} %bitcast.6, f32[1,2048]{1,0:T(1,128)} %bitcast.7, f32[1,2048]{1,0:T(1,128)} %bitcast.8, bf16[24576,128]{1,0:T(8,128)(2,1)} %bitcast.5), custom_call_target="tpu_custom_call" | custom-call | tf_op jit(solution)/shard_map/analyse/pallas_call | solution.py:418
  47.7 6.7 %blend.1 = bf16[24576,128]{1,0:T(8,128)(2,1)} custom-call(bf16[9,80,128]{2,1,0:T(8,128)(2,1)} %get-tuple-element.7.blend_any, bf16[24576,128]{1,0:T(8,128)(2,1)} %get-tuple-element.8.ens_any), custom_call_target="tpu_custom_call" | custom-call | tf_op jit(solution)/shard_map/blend/pallas_call | solution.py:468

commit v5 on v4

--- a/solution.py
+++ b/solution.py
@@ -14,7 +14,6 @@
 OBS = 2048
 NEWTON = 6
 ITERS = 2
-PACK = 72
 QUART = 512
 GROUP = 8
 UNROLL = 4
@@ -91,38 +90,40 @@
     return jnp.sum(jnp.where(row == col, matrix, 0.0), axis=0, keepdims=True)
 
 
-def pack_stats(total):
-    gram = total[:K]
-    tail_row, _ = iotas((PACK - K // 2, K))
-    tail = jnp.where(tail_row == 0, diagonal_of(gram), total[K : K + 1])
-    return jnp.concatenate([fold(gram), tail], axis=0)
-
-
-def unpack_stats(packed):
+def opened(symmetric, line):
+    tail_row, _ = iotas((PACKED - K // 2, K))
+    tail = jnp.where(tail_row == 0, diagonal_of(symmetric), jnp.where(tail_row == 2, line, 0.0))
+    return jnp.concatenate([fold(symmetric), tail], axis=0)
+
+
+def lines_of(packed):
     half = K // 2
-    return unfold(packed[:half], packed[half : half + 1]), packed[half + 1 : half + 2]
-
-
-def pack_transform(spread, weights):
+    diagonal = packed[half : half + 1] + packed[half + 1 : half + 2]
+    return diagonal, packed[half + 2 : half + 3] + packed[half + 3 : half + 4]
+
+
+def closed(packed):
     tail_row, _ = iotas((PACKED - K // 2, K))
     tail = jnp.zeros((PACKED - K // 2, K), F32)
-    for k, line in enumerate((diagonal_of(spread), weights)):
+    for k, line in enumerate(lines_of(packed)):
         high, low = split(line)
         tail = jnp.where(tail_row == 2 * k, high.astype(F32), tail)
         tail = jnp.where(tail_row == 2 * k + 1, low.astype(F32), tail)
-    return jnp.concatenate([fold(spread), tail], axis=0).astype(BF16)
+    return jnp.concatenate([packed[: K // 2], tail], axis=0).astype(BF16)
+
+
+def unpack(packed):
+    diagonal, line = lines_of(packed)
+    return unfold(packed[: K // 2], diagonal), line
 
 
 def unpack_transform(packed):
-    half = K // 2
-    packed = packed.astype(F32)
-    diagonal = packed[half : half + 1] + packed[half + 1 : half + 2]
-    weights = packed[half + 2 : half + 3] + packed[half + 3 : half + 4]
-    return (weights + unfold(packed[:half], diagonal)).astype(BF16)
+    spread, weights = unpack(packed.astype(F32))
+    return (weights + spread).astype(BF16)
 
 
 def transform_parts(packed):
-    gram, projected = unpack_stats(packed)
+    gram, projected = unpack(packed)
     row, col = iotas((K, K))
     identity = jnp.where(row == col, 1.0, 0.0).astype(F32)
     system = gram + (K - 1) * identity
@@ -287,11 +288,10 @@
         while pending:
             pending.pop().wait_send()
 
-    def weighted(t, sent, got, copies):
-        total = sent[t]
+    def weighted(t, total, got, copies):
         for k in reversed(range(4)):
             copies[STAT_STEPS.index(-STAT_STEPS[k])].wait_recv()
-            total = total + STAT_WEIGHTS[k] * got[t, k]
+            total = total + STAT_WEIGHTS[k] * got[t, k].astype(F32)
         pending.extend(copies)
         return total
 
@@ -330,7 +330,8 @@
                 fresh = fresh.astype(BF16).astype(F32)
                 centre = jnp.sum(fresh, axis=0, keepdims=True) * (1.0 / K)
                 total = accumulate(total, lanes, fresh - centre, centre)
-        stat_x[t] = pack_stats(total)
+        own = opened(total[:K], total[K : K + 1])
+        stat_x[t] = closed(own)
 
         if t == 0:
             pl.semaphore_wait(barrier, len(partners))
@@ -341,14 +342,15 @@
             matrices[...] = full_matrices(transforms[...])
             apply_some(0, CX // 2)
             settle()
-        stat_y[t] = weighted(t, stat_x, got_x, copies)
+        own = weighted(t, own, got_x, copies)
+        stat_y[t] = closed(own)
         copies = exchange(t, stat_y, got_y, send_y, recv_y, lambda step: (0, step))
         for copy in copies:
             copy.start()
         if t == 1:
             apply_some(CX // 2, CX)
-        spread, weights = transform_parts(weighted(t, stat_y, got_y, copies))
-        own_ref[t] = pack_transform(spread, weights)
+        spread, weights = transform_parts(weighted(t, own, got_y, copies))
+        own_ref[t] = closed(opened(spread, weights))
         landing = nearby if t == 0 else blend_ref
         copies = {}
         for k, (a, b) in enumerate(BLEND_STEPS):
@@ -436,10 +438,10 @@
             pltpu.VMEM((K, OBS), BF16),
             pltpu.VMEM((9 * K, K), F32),
             pltpu.VMEM((2, 3 * K, 2 * K), BF16),
-            pltpu.VMEM((ITERS, PACK, K), F32),
-            pltpu.VMEM((ITERS, PACK, K), F32),
-            pltpu.VMEM((ITERS, 4, PACK, K), F32),
-            pltpu.VMEM((ITERS, 4, PACK, K), F32),
+            pltpu.VMEM((ITERS, PACKED, K), BF16),
+            pltpu.VMEM((ITERS, PACKED, K), BF16),
+            pltpu.VMEM((ITERS, 4, PACKED, K), BF16),
+            pltpu.VMEM((ITERS, 4, PACKED, K), BF16),
             pltpu.VMEM((9, PACKED, K), BF16),
             pltpu.VMEM((9 * K, K), BF16),
             pltpu.VMEM((ITERS, PACKED, K), BF16),

time: 54.5 us -> 52.4 us (0.961)
  Pallas kernels: 54.4 us -> 52.3 us
    pallas_call x1, Pallas kernels: 47.7 us -> 45.6 us  [shards(): pl.pallas_call(first_kernel, out_shape=(jax.ShapeDtypeStruct((ROWS, K), B...]
where the time goes in v5:
time: 52.4 us; the launch traced here: 52.3 us
  Pallas kernels  52.3 us (100%)
    pallas_call x1, Pallas kernels, shards(): pl.pallas_call(first_kernel, out_shape=(jax.ShapeDtypeStruct((ROWS, K), B...  45.6 us
    pallas_call x1, Pallas kernels, shards(): pl.pallas_call(last_kernel, out_shape=jax.ShapeDtypeStruct((ROWS, K), BF1...  6.7 us

profile of v5, /device:TPU:1, one launch (start us, length us, event | category | flops | bytes accessed | tf_op | source)
XLA Modules:
  0.0 52.3 jit_solution(13254207814938939882)
XLA Ops:
  0.0 45.6 %analyse.1 = (bf16[24576,128]{1,0:T(8,128)(2,1)}, bf16[9,80,128]{2,1,0:T(8,128)(2,1)}) custom-call(s32[8,16]{1,0:T(8,128)} %count_any.1, s32[1,2048]{1,0:T(1,128)} %bitcast.6, f32[1,2048]{1,0:T(1,128)} %bitcast.7, f32[1,2048]{1,0:T(1,128)} %bitcast.8, bf16[24576,128]{1,0:T(8,128)(2,1)} %bitcast.5), custom_call_target="tpu_custom_call" | custom-call | tf_op jit(solution)/shard_map/analyse/pallas_call | solution.py:420
  45.6 6.7 %blend.1 = bf16[24576,128]{1,0:T(8,128)(2,1)} custom-call(bf16[9,80,128]{2,1,0:T(8,128)(2,1)} %get-tuple-element.7.blend_any, bf16[24576,128]{1,0:T(8,128)(2,1)} %get-tuple-element.8.ens_any), custom_call_target="tpu_custom_call" | custom-call | tf_op jit(solution)/shard_map/blend/pallas_call | solution.py:470

commit v6 on v5

--- a/solution.py
+++ b/solution.py
@@ -204,10 +204,10 @@
 
 def first_kernel(
     count_any, cell_any, value_any, weight_any, ens_any,
-    next_ref, blend_ref,
-    count_ref, cell_ref, given, cells_ref, ens, applied, ens32, picked, rows, deviations, matrices, stationary,
+    applied, blend_ref,
+    count_ref, cell_ref, given, cells_ref, ens, ens32, picked, rows, deviations, matrices, stationary,
     stat_x, stat_y, got_x, got_y, nearby, transforms, own_ref,
-    small_sem, load_sem, store_sem, own_sem, send_x, recv_x, send_y, recv_y, send_t, recv_t,
+    small_sem, load_sem, own_sem, send_x, recv_x, send_y, recv_y, send_t, recv_t,
 ):
     gx, gy = lax.axis_index("gx"), lax.axis_index("gy")
     nx, ny = lax.axis_size("gx"), lax.axis_size("gy")
@@ -298,11 +298,8 @@
     def nothing(i):
         pass
 
-    def store(i):
-        pltpu.make_async_copy(column(applied, i), column(next_ref, i), store_sem.at[i]).start()
-
     def apply_some(first, last):
-        apply_columns(first, last, matrices, stationary, ens, applied, nothing, store)
+        apply_columns(first, last, matrices, stationary, ens, applied, nothing, nothing)
 
     for t in range(ITERS):
         total = jnp.zeros((K + 16, K), F32)
@@ -374,39 +371,28 @@
             settle()
         for step in reversed(BLEND_STEPS):
             copies[step].wait_recv()
-            if t == 0:
+        if t == 0:
+            for step in BLEND_STEPS:
                 slot = slot_of(*step)
                 transforms[slot * K : (slot + 1) * K] = unpack_transform(nearby[slot])
-        if t == 1:
+        else:
             mine.wait()
         pending.extend(copies.values())
     settle()
 
-    @pl.loop(0, CX)
-    def _(i):
-        pltpu.make_async_copy(column(applied, i), column(next_ref, i), store_sem.at[i]).wait()
-
-
-def last_kernel(blend_any, ens_any, out_any, nearby, ens, applied, transforms, matrices, stationary, blend_sem, load_sem, store_sem):
-    get = pltpu.make_async_copy(blend_any, nearby, blend_sem)
-    get.start()
-
-    @pl.loop(0, CX)
-    def _(i):
-        pltpu.make_async_copy(column(ens_any, i), column(ens, i), load_sem.at[i]).start()
-
-    get.wait()
+
+def last_kernel(nearby, ens, out_any, applied, transforms, matrices, stationary, store_sem):
     for slot in range(9):
         transforms[slot * K : (slot + 1) * K] = unpack_transform(nearby[slot])
     matrices[...] = full_matrices(transforms[...])
 
-    def load(i):
-        pltpu.make_async_copy(column(ens_any, i), column(ens, i), load_sem.at[i]).wait()
+    def nothing(i):
+        pass
 
     def store(i):
         pltpu.make_async_copy(column(applied, i), column(out_any, i), store_sem.at[i]).start()
 
-    apply_columns(0, CX, matrices, stationary, ens, applied, load, store)
+    apply_columns(0, CX, matrices, stationary, ens, applied, nothing, store)
 
     @pl.loop(0, CX)
     def _(i):
@@ -416,6 +402,7 @@
 def shards(ensemble, obs_cell, obs_value, obs_weight, obs_count):
     flat = ensemble.reshape(ROWS, K)
     anywhere = pl.BlockSpec(memory_space=pl.ANY)
+    fixed = pl.BlockSpec(memory_space=pltpu.HBM)
     dma = pltpu.SemaphoreType.DMA
     following, blend = pl.pallas_call(
         first_kernel,
@@ -423,14 +410,13 @@
             jax.ShapeDtypeStruct((ROWS, K), BF16),
             jax.ShapeDtypeStruct((9, PACKED, K), BF16),
         ),
-        in_specs=[anywhere] * 5,
-        out_specs=(anywhere, anywhere),
+        in_specs=[fixed] * 5,
+        out_specs=(pl.BlockSpec(memory_space=pltpu.VMEM), anywhere),
         scratch_shapes=[
             pltpu.SMEM((BX, BY), jnp.int32),
             pltpu.SMEM((1, OBS), jnp.int32),
             pltpu.VMEM((2, 1, OBS), F32),
             pltpu.VMEM((1, OBS), jnp.int32),
-            pltpu.VMEM((ROWS, K), BF16),
             pltpu.VMEM((ROWS, K), BF16),
             pltpu.VMEM((ROWS, K), F32),
             pltpu.VMEM((OBS, K), F32),
@@ -447,7 +433,6 @@
             pltpu.VMEM((ITERS, PACKED, K), BF16),
             dma((5,)),
             dma((CX,)),
-            dma((CX,)),
             dma(()),
             dma((ITERS, 4)),
             dma((ITERS, 4)),
@@ -457,33 +442,34 @@
             dma((ITERS, 9)),
         ],
         compiler_params=pltpu.CompilerParams(
-            collective_id=0, has_side_effects=True, vmem_limit_bytes=58 * 1024 * 1024
+            collective_id=0, has_side_effects=True, vmem_limit_bytes=44 * 1024 * 1024
         ),
         name="analyse",
     )(
-        obs_count,
-        obs_cell.reshape(1, OBS),
-        obs_value.reshape(1, OBS),
-        obs_weight.reshape(1, OBS),
-        flat,
+        *(
+            pltpu.with_memory_space_constraint(array, pltpu.HBM)
+            for array in (
+                obs_count,
+                obs_cell.reshape(1, OBS),
+                obs_value.reshape(1, OBS),
+                obs_weight.reshape(1, OBS),
+                flat,
+            )
+        )
     )
     out = pl.pallas_call(
         last_kernel,
         out_shape=jax.ShapeDtypeStruct((ROWS, K), BF16),
-        in_specs=[anywhere] * 2,
-        out_specs=anywhere,
+        in_specs=[pl.BlockSpec(memory_space=pltpu.VMEM)] * 2,
+        out_specs=fixed,
         scratch_shapes=[
-            pltpu.VMEM((9, PACKED, K), BF16),
-            pltpu.VMEM((ROWS, K), BF16),
             pltpu.VMEM((ROWS, K), BF16),
             pltpu.VMEM((9 * K, K), BF16),
             pltpu.VMEM((9 * K, K), F32),
             pltpu.VMEM((2, 3 * K, 2 * K), BF16),
-            dma(()),
-            dma((CX,)),
             dma((CX,)),
         ],
-        compiler_params=pltpu.CompilerParams(vmem_limit_bytes=58 * 1024 * 1024),
+        compiler_params=pltpu.CompilerParams(vmem_limit_bytes=44 * 1024 * 1024),
         name="blend",
     )(blend, following)
     return out.reshape(ensemble.shape)

time: 52.4 us -> 50.6 us (0.966)
  Pallas kernels: 52.3 us -> 50.5 us
    pallas_call x1, Pallas kernels: 6.7 us -> 5.57 us  [shards(): pl.pallas_call(last_kernel, out_shape=jax.ShapeDtypeStruct((ROWS, K), BF1...]
    pallas_call x1, Pallas kernels: 45.6 us -> 45 us  [shards(): pl.pallas_call(first_kernel, out_shape=(jax.ShapeDtypeStruct((ROWS, K), B...]
where the time goes in v6:
time: 50.6 us; the launch traced here: 50.5 us
  Pallas kernels  50.5 us (100%)
    pallas_call x1, Pallas kernels, shards(): pl.pallas_call(first_kernel, out_shape=(jax.ShapeDtypeStruct((ROWS, K), B...  45 us
    pallas_call x1, Pallas kernels, shards(): pl.pallas_call(last_kernel, out_shape=jax.ShapeDtypeStruct((ROWS, K), BF1...  5.57 us

profile of v6, /device:TPU:1, one launch (start us, length us, event | category | flops | bytes accessed | tf_op | source)
XLA Modules:
  0.0 50.5 jit_solution(15298300127746078425)
XLA Ops:
  0.0 45.0 %analyse.1 = (bf16[24576,128]{1,0:T(8,128)(2,1)S(1)}, bf16[9,80,128]{2,1,0:T(8,128)(2,1)S(1)}) custom-call(s32[8,16]{1,0:T(8,128)} %count_any.1, s32[1,2048]{1,0:T(1,128)} %bitcast.6, f32[1,2048]{1,0:T(1,128)} %bitcast.7, f32[1,2048]{1,0:T(1,128)} %bitcast.8, bf16[24576,128]{1,0:T(8,128)(2,1)} %bitcast.5), custom_call_target="tpu_custom_call" | custom-call | tf_op jit(solution)/shard_map/analyse/pallas_call | solution.py:407
  45.0 5.6 %blend.1 = bf16[24576,128]{1,0:T(8,128)(2,1)} custom-call(bf16[9,80,128]{2,1,0:T(8,128)(2,1)S(1)} %get-tuple-element.7.nearby, bf16[24576,128]{1,0:T(8,128)(2,1)S(1)} %get-tuple-element.8.ens), custom_call_target="tpu_custom_call" | custom-call | tf_op jit(solution)/shard_map/blend/pallas_call | solution.py:460

commit v7 on v6

--- a/solution.py
+++ b/solution.py
@@ -15,6 +15,7 @@
 NEWTON = 6
 ITERS = 2
 QUART = 512
+PART = 256
 GROUP = 8
 UNROLL = 4
 GATHER = 64
@@ -205,7 +206,7 @@
 def first_kernel(
     count_any, cell_any, value_any, weight_any, ens_any,
     applied, blend_ref,
-    count_ref, cell_ref, given, cells_ref, ens, ens32, picked, rows, deviations, matrices, stationary,
+    count_ref, cell_ref, given, cells_ref, ens, ens32, picked, rows, deviations, scaled, matrices, stationary,
     stat_x, stat_y, got_x, got_y, nearby, transforms, own_ref,
     small_sem, load_sem, own_sem, send_x, recv_x, send_y, recv_y, send_t, recv_t,
 ):
@@ -244,9 +245,9 @@
     rows[1:2] = given[0]
     east = jnp.floor((cells + 0.5) * (1.0 / XROWS))
     north = jnp.floor((cells - XROWS * east + 0.5) * (1.0 / LEV))
-    for first, hat in ((2, hats((east + 0.5) / CX)), (5, hats((north + 0.5) / CY))):
-        for k in range(3):
-            rows[first + k : first + k + 1] = hat[k]
+    hat_x, hat_y = hats((east + 0.5) / CX), hats((north + 0.5) / CY)
+    for slot in range(9):
+        rows[3 + slot : 4 + slot] = hat_x[slot // 3] * hat_y[slot % 3]
 
     @pl.loop(0, CX)
     def _(i):
@@ -311,19 +312,12 @@
                 lanes = slice(q * QUART, (q + 1) * QUART)
                 moved = mm_nt(centre_rows, picked[lanes].astype(BF16))
                 total = accumulate(total, lanes, moved[:K], moved[K : K + 1])
-                deviations[:, lanes] = moved[:K].astype(BF16)
-                rows[8:9, lanes] = moved[K : K + 1]
+                deviations[:, lanes] = moved[:K]
+                rows[2:3, lanes] = moved[K : K + 1]
         else:
             for q in range(OBS // QUART):
                 lanes = slice(q * QUART, (q + 1) * QUART)
-                out = mm(transforms[...], deviations[:, lanes])
-                fresh = rows[8:9, lanes]
-                for a in range(3):
-                    at_a = a * 3 * K
-                    part = rows[5:6, lanes] * out[at_a : at_a + K]
-                    part = part + rows[6:7, lanes] * out[at_a + K : at_a + 2 * K]
-                    part = part + rows[7:8, lanes] * out[at_a + 2 * K : at_a + 3 * K]
-                    fresh = fresh + rows[2 + a : 3 + a, lanes] * part
+                fresh = rows[2:3, lanes] + mm(transforms[...], scaled[:, lanes])
                 fresh = fresh.astype(BF16).astype(F32)
                 centre = jnp.sum(fresh, axis=0, keepdims=True) * (1.0 / K)
                 total = accumulate(total, lanes, fresh - centre, centre)
@@ -336,13 +330,14 @@
         for copy in copies:
             copy.start()
         if t == 1:
-            matrices[...] = full_matrices(transforms[...])
+            for slot in range(9):
+                matrices[slot * K : (slot + 1) * K] = full_matrices(transforms[:, slot * K : (slot + 1) * K])
             apply_some(0, CX // 2)
             settle()
         own = weighted(t, own, got_x, copies)
         stat_y[t] = closed(own)
         copies = exchange(t, stat_y, got_y, send_y, recv_y, lambda step: (0, step))
-        for copy in copies:
+        for copy in reversed(copies):
             copy.start()
         if t == 1:
             apply_some(CX // 2, CX)
@@ -364,7 +359,15 @@
             copy.start()
         own = slot_of(0, 0)
         if t == 0:
-            transforms[own * K : (own + 1) * K] = (weights + spread).astype(BF16)
+            transforms[:, own * K : (own + 1) * K] = (weights + spread).astype(BF16)
+
+            @pl.loop(0, OBS // PART)
+            def _(q):
+                lanes = pl.ds(pl.multiple_of(q * PART, PART), PART)
+                for slot in range(9):
+                    part = rows[3 + slot : 4 + slot, lanes] * deviations[:, lanes]
+                    scaled[slot * K : (slot + 1) * K, lanes] = part.astype(BF16)
+
         else:
             mine = pltpu.make_async_copy(own_ref.at[t], landing.at[own], own_sem)
             mine.start()
@@ -374,7 +377,7 @@
         if t == 0:
             for step in BLEND_STEPS:
                 slot = slot_of(*step)
-                transforms[slot * K : (slot + 1) * K] = unpack_transform(nearby[slot])
+                transforms[:, slot * K : (slot + 1) * K] = unpack_transform(nearby[slot])
         else:
             mine.wait()
         pending.extend(copies.values())
@@ -421,7 +424,8 @@
             pltpu.VMEM((ROWS, K), F32),
             pltpu.VMEM((OBS, K), F32),
             pltpu.VMEM((16, OBS), F32),
-            pltpu.VMEM((K, OBS), BF16),
+            pltpu.VMEM((K, OBS), F32),
+            pltpu.VMEM((9 * K, OBS), BF16),
             pltpu.VMEM((9 * K, K), F32),
             pltpu.VMEM((2, 3 * K, 2 * K), BF16),
             pltpu.VMEM((ITERS, PACKED, K), BF16),
@@ -429,7 +433,7 @@
             pltpu.VMEM((ITERS, 4, PACKED, K), BF16),
             pltpu.VMEM((ITERS, 4, PACKED, K), BF16),
             pltpu.VMEM((9, PACKED, K), BF16),
-            pltpu.VMEM((9 * K, K), BF16),
+            pltpu.VMEM((K, 9 * K), BF16),
             pltpu.VMEM((ITERS, PACKED, K), BF16),
             dma((5,)),
             dma((CX,)),

time: 50.6 us -> 49.5 us (0.978)
  Pallas kernels: 50.5 us -> 49.1 us
    pallas_call x1, Pallas kernels: 45 us -> 43.5 us  [shards(): pl.pallas_call(first_kernel, out_shape=(jax.ShapeDtypeStruct((ROWS, K), B...]
where the time goes in v7:
time: 49.5 us; the launch traced here: 49.1 us
  Pallas kernels  49.1 us (99%)
    pallas_call x1, Pallas kernels, shards(): pl.pallas_call(first_kernel, out_shape=(jax.ShapeDtypeStruct((ROWS, K), B...  43.5 us
    pallas_call x1, Pallas kernels, shards(): pl.pallas_call(last_kernel, out_shape=jax.ShapeDtypeStruct((ROWS, K), BF1...  5.57 us

profile of v7, /device:TPU:1, one launch (start us, length us, event | category | flops | bytes accessed | tf_op | source)
XLA Modules:
  0.0 49.1 jit_solution(5504556384155802301)
XLA Ops:
  0.0 43.5 %analyse.1 = (bf16[24576,128]{1,0:T(8,128)(2,1)S(1)}, bf16[9,80,128]{2,1,0:T(8,128)(2,1)S(1)}) custom-call(s32[8,16]{1,0:T(8,128)} %count_any.1, s32[1,2048]{1,0:T(1,128)} %bitcast.6, f32[1,2048]{1,0:T(1,128)} %bitcast.7, f32[1,2048]{1,0:T(1,128)} %bitcast.8, bf16[24576,128]{1,0:T(8,128)(2,1)} %bitcast.5), custom_call_target="tpu_custom_call" | custom-call | tf_op jit(solution)/shard_map/analyse/pallas_call | solution.py:410
  43.5 5.6 %blend.1 = bf16[24576,128]{1,0:T(8,128)(2,1)} custom-call(bf16[9,80,128]{2,1,0:T(8,128)(2,1)S(1)} %get-tuple-element.7.nearby, bf16[24576,128]{1,0:T(8,128)(2,1)S(1)} %get-tuple-element.8.ens), custom_call_target="tpu_custom_call" | custom-call | tf_op jit(solution)/shard_map/blend/pallas_call | solution.py:464

commit v8 on v7

--- a/solution.py
+++ b/solution.py
@@ -18,6 +18,7 @@
 PART = 256
 GROUP = 8
 UNROLL = 4
+SLOTS = 4
 GATHER = 64
 PACKED = 80
 BX = 8
@@ -156,13 +157,22 @@
 
 
 def blend_column(i, slot, matrices, stationary):
-    weights = hats((i.astype(F32) + 0.5) / CX)
+    static = isinstance(i, int)
+    weights = hat_of(i, CX) if static else hats((i.astype(F32) + 0.5) / CX)
     for b in range(3):
-        blend = weights[0] * matrices[b * K : (b + 1) * K]
-        for a in (1, 2):
+        blend = None
+        for a in range(3):
+            if static and weights[a] == 0.0:
+                continue
             at = (a * 3 + b) * K
-            blend = blend + weights[a] * matrices[at : at + K]
+            term = weights[a] * matrices[at : at + K]
+            blend = term if blend is None else blend + term
         stationary[slot, b * K : (b + 1) * K] = wide(blend)
+
+
+def row_of(i, offset=0):
+    row = i * XROWS + offset
+    return row if isinstance(i, int) else pl.multiple_of(row, 16)
 
 
 def apply_column(i, slot, ens, fresh, stationary):
@@ -170,7 +180,7 @@
         matrix = stationary[slot, half * K : half * K + 2 * K]
         for group in range(CY // 2 // GROUP):
             first = half * (CY // 2) + group * GROUP
-            here = pl.ds(pl.multiple_of(i * XROWS + first * LEV, 16), GROUP * LEV)
+            here = pl.ds(row_of(i, first * LEV), GROUP * LEV)
             block = ens[here]
             out = mm_nt(jnp.concatenate([block, block], axis=1), matrix)
             parts = []
@@ -181,17 +191,14 @@
             fresh[here] = jnp.concatenate(parts, axis=0).astype(BF16)
 
 
-def apply_columns(first, last, matrices, stationary, ens, fresh, before, after):
+def apply_columns(first, last, matrices, stationary, ens, fresh):
     blend_column(jnp.int32(first), 0, matrices, stationary)
 
     @pl.loop(first // UNROLL, last // UNROLL)
     def _(step):
         for k in range(UNROLL):
-            before(step * UNROLL + k)
-        for k in range(UNROLL):
             i = step * UNROLL + k
             apply_column(i, k % 2, ens, fresh, stationary)
-            after(i)
             blend_column(jnp.minimum(i + 1, CX - 1), 1 - k % 2, matrices, stationary)
 
 
@@ -200,7 +207,7 @@
 
 
 def column(ref, i):
-    return ref.at[pl.ds(pl.multiple_of(i * XROWS, XROWS), XROWS)]
+    return ref.at[pl.ds(row_of(i), XROWS)]
 
 
 def first_kernel(
@@ -296,11 +303,8 @@
         pending.extend(copies)
         return total
 
-    def nothing(i):
-        pass
-
     def apply_some(first, last):
-        apply_columns(first, last, matrices, stationary, ens, applied, nothing, nothing)
+        apply_columns(first, last, matrices, stationary, ens, applied)
 
     for t in range(ITERS):
         total = jnp.zeros((K + 16, K), F32)
@@ -384,22 +388,26 @@
     settle()
 
 
-def last_kernel(nearby, ens, out_any, applied, transforms, matrices, stationary, store_sem):
-    for slot in range(9):
-        transforms[slot * K : (slot + 1) * K] = unpack_transform(nearby[slot])
-    matrices[...] = full_matrices(transforms[...])
-
-    def nothing(i):
-        pass
+def last_kernel(nearby, ens, out_any, applied, matrices, stationary, store_sem):
+    def ready(slots):
+        for slot in slots:
+            matrices[slot * K : (slot + 1) * K] = full_matrices(unpack_transform(nearby[slot]))
 
     def store(i):
-        pltpu.make_async_copy(column(applied, i), column(out_any, i), store_sem.at[i]).start()
-
-    apply_columns(0, CX, matrices, stationary, ens, applied, nothing, store)
-
-    @pl.loop(0, CX)
-    def _(i):
-        pltpu.make_async_copy(column(applied, i), column(out_any, i), store_sem.at[i]).wait()
+        return pltpu.make_async_copy(column(applied, i), column(out_any, i), store_sem.at[i])
+
+    ready(range(6))
+    blend_column(0, 0, matrices, stationary)
+    for i in range(CX):
+        apply_column(i, i % SLOTS, ens, applied, stationary)
+        if i + 1 < CX:
+            blend_column(i + 1, (i + 1) % SLOTS, matrices, stationary)
+        store(i).start()
+        if i == 1:
+            ready(range(6, 9))
+
+    for i in range(CX):
+        store(i).wait()
 
 
 def shards(ensemble, obs_cell, obs_value, obs_weight, obs_count):
@@ -468,9 +476,8 @@
         out_specs=fixed,
         scratch_shapes=[
             pltpu.VMEM((ROWS, K), BF16),
-            pltpu.VMEM((9 * K, K), BF16),
             pltpu.VMEM((9 * K, K), F32),
-            pltpu.VMEM((2, 3 * K, 2 * K), BF16),
+            pltpu.VMEM((SLOTS, 3 * K, 2 * K), BF16),
             dma((CX,)),
         ],
         compiler_params=pltpu.CompilerParams(vmem_limit_bytes=44 * 1024 * 1024),

time: 49.5 us -> 48.9 us (0.988)
  Pallas kernels: 49.1 us -> 48.4 us
    pallas_call x1, Pallas kernels: 5.57 us -> 4.9 us  [shards(): pl.pallas_call(last_kernel, out_shape=jax.ShapeDtypeStruct((ROWS, K), BF1...]
where the time goes in v8:
time: 48.9 us; the launch traced here: 48.4 us
  Pallas kernels  48.4 us (99%)
    pallas_call x1, Pallas kernels, shards(): pl.pallas_call(first_kernel, out_shape=(jax.ShapeDtypeStruct((ROWS, K), B...  43.5 us
    pallas_call x1, Pallas kernels, shards(): pl.pallas_call(last_kernel, out_shape=jax.ShapeDtypeStruct((ROWS, K), BF1...  4.9 us

profile of v8, /device:TPU:1, one launch (start us, length us, event | category | flops | bytes accessed | tf_op | source)
XLA Modules:
  0.0 48.4 jit_solution(1420665350249215852)
XLA Ops:
  0.0 43.5 %analyse.1 = (bf16[24576,128]{1,0:T(8,128)(2,1)S(1)}, bf16[9,80,128]{2,1,0:T(8,128)(2,1)S(1)}) custom-call(s32[8,16]{1,0:T(8,128)} %count_any.1, s32[1,2048]{1,0:T(1,128)} %bitcast.6, f32[1,2048]{1,0:T(1,128)} %bitcast.7, f32[1,2048]{1,0:T(1,128)} %bitcast.8, bf16[24576,128]{1,0:T(8,128)(2,1)} %bitcast.5), custom_call_target="tpu_custom_call" | custom-call | tf_op jit(solution)/shard_map/analyse/pallas_call | solution.py:418
  43.5 4.9 %blend.1 = bf16[24576,128]{1,0:T(8,128)(2,1)} custom-call(bf16[9,80,128]{2,1,0:T(8,128)(2,1)S(1)} %get-tuple-element.7.nearby, bf16[24576,128]{1,0:T(8,128)(2,1)S(1)} %get-tuple-element.8.ens), custom_call_target="tpu_custom_call" | custom-call | tf_op jit(solution)/shard_map/blend/pallas_call | solution.py:472

commit v9 on v8

--- a/solution.py
+++ b/solution.py
@@ -156,7 +156,7 @@
     return below, 1.0 - below - above, above
 
 
-def blend_column(i, slot, matrices, stationary):
+def blend_column(i, slot, matrix_of, stationary):
     static = isinstance(i, int)
     weights = hat_of(i, CX) if static else hats((i.astype(F32) + 0.5) / CX)
     for b in range(3):
@@ -164,8 +164,7 @@
         for a in range(3):
             if static and weights[a] == 0.0:
                 continue
-            at = (a * 3 + b) * K
-            term = weights[a] * matrices[at : at + K]
+            term = weights[a] * matrix_of(a * 3 + b)
             blend = term if blend is None else blend + term
         stationary[slot, b * K : (b + 1) * K] = wide(blend)
 
@@ -191,15 +190,15 @@
             fresh[here] = jnp.concatenate(parts, axis=0).astype(BF16)
 
 
-def apply_columns(first, last, matrices, stationary, ens, fresh):
-    blend_column(jnp.int32(first), 0, matrices, stationary)
+def apply_columns(first, last, matrix_of, stationary, ens, fresh):
+    blend_column(jnp.int32(first), 0, matrix_of, stationary)
 
     @pl.loop(first // UNROLL, last // UNROLL)
     def _(step):
         for k in range(UNROLL):
             i = step * UNROLL + k
             apply_column(i, k % 2, ens, fresh, stationary)
-            blend_column(jnp.minimum(i + 1, CX - 1), 1 - k % 2, matrices, stationary)
+            blend_column(jnp.minimum(i + 1, CX - 1), 1 - k % 2, matrix_of, stationary)
 
 
 def full_matrices(transforms):
@@ -212,7 +211,7 @@
 
 def first_kernel(
     count_any, cell_any, value_any, weight_any, ens_any,
-    applied, blend_ref,
+    applied, blend_ref, middle_ref,
     count_ref, cell_ref, given, cells_ref, ens, ens32, picked, rows, deviations, scaled, matrices, stationary,
     stat_x, stat_y, got_x, got_y, nearby, transforms, own_ref,
     small_sem, load_sem, own_sem, send_x, recv_x, send_y, recv_y, send_t, recv_t,
@@ -304,7 +303,7 @@
         return total
 
     def apply_some(first, last):
-        apply_columns(first, last, matrices, stationary, ens, applied)
+        apply_columns(first, last, lambda slot: matrices[slot * K : (slot + 1) * K], stationary, ens, applied)
 
     for t in range(ITERS):
         total = jnp.zeros((K + 16, K), F32)
@@ -376,19 +375,30 @@
             mine = pltpu.make_async_copy(own_ref.at[t], landing.at[own], own_sem)
             mine.start()
             settle()
-        for step in reversed(BLEND_STEPS):
+        near, far = BLEND_STEPS[6:], BLEND_STEPS[:6]
+        for step in near:
+            copies[step].wait_recv()
+        if t == 1:
+            mine.wait()
+            middle_ref[K : 2 * K] = full_matrices((weights + spread).astype(BF16))
+        for step in near:
+            slot = slot_of(*step)
+            if t == 0:
+                transforms[:, slot * K : (slot + 1) * K] = unpack_transform(nearby[slot])
+            else:
+                here = (step[1] + 1) * K
+                middle_ref[here : here + K] = full_matrices(unpack_transform(blend_ref[slot]))
+        for step in far:
             copies[step].wait_recv()
         if t == 0:
-            for step in BLEND_STEPS:
+            for step in far:
                 slot = slot_of(*step)
                 transforms[:, slot * K : (slot + 1) * K] = unpack_transform(nearby[slot])
-        else:
-            mine.wait()
         pending.extend(copies.values())
     settle()
 
 
-def last_kernel(nearby, ens, out_any, applied, matrices, stationary, store_sem):
+def last_kernel(nearby, middle, ens, out_any, applied, matrices, stationary, store_sem):
     def ready(slots):
         for slot in slots:
             matrices[slot * K : (slot + 1) * K] = full_matrices(unpack_transform(nearby[slot]))
@@ -396,12 +406,17 @@
     def store(i):
         return pltpu.make_async_copy(column(applied, i), column(out_any, i), store_sem.at[i])
 
-    ready(range(6))
-    blend_column(0, 0, matrices, stationary)
+    def matrix_of(slot):
+        if 3 <= slot < 6:
+            return middle[(slot - 3) * K : (slot - 2) * K]
+        return matrices[slot * K : (slot + 1) * K]
+
+    ready(range(3))
+    blend_column(0, 0, matrix_of, stationary)
     for i in range(CX):
         apply_column(i, i % SLOTS, ens, applied, stationary)
         if i + 1 < CX:
-            blend_column(i + 1, (i + 1) % SLOTS, matrices, stationary)
+            blend_column(i + 1, (i + 1) % SLOTS, matrix_of, stationary)
         store(i).start()
         if i == 1:
             ready(range(6, 9))
@@ -415,14 +430,15 @@
     anywhere = pl.BlockSpec(memory_space=pl.ANY)
     fixed = pl.BlockSpec(memory_space=pltpu.HBM)
     dma = pltpu.SemaphoreType.DMA
-    following, blend = pl.pallas_call(
+    following, blend, middle = pl.pallas_call(
         first_kernel,
         out_shape=(
             jax.ShapeDtypeStruct((ROWS, K), BF16),
             jax.ShapeDtypeStruct((9, PACKED, K), BF16),
+            jax.ShapeDtypeStruct((3 * K, K), F32),
         ),
         in_specs=[fixed] * 5,
-        out_specs=(pl.BlockSpec(memory_space=pltpu.VMEM), anywhere),
+        out_specs=(pl.BlockSpec(memory_space=pltpu.VMEM),) * 3,
         scratch_shapes=[
             pltpu.SMEM((BX, BY), jnp.int32),
             pltpu.SMEM((1, OBS), jnp.int32),
@@ -472,7 +488,7 @@
     out = pl.pallas_call(
         last_kernel,
         out_shape=jax.ShapeDtypeStruct((ROWS, K), BF16),
-        in_specs=[pl.BlockSpec(memory_space=pltpu.VMEM)] * 2,
+        in_specs=[pl.BlockSpec(memory_space=pltpu.VMEM)] * 3,
         out_specs=fixed,
         scratch_shapes=[
             pltpu.VMEM((ROWS, K), BF16),
@@ -482,7 +498,7 @@
         ],
         compiler_params=pltpu.CompilerParams(vmem_limit_bytes=44 * 1024 * 1024),
         name="blend",
-    )(blend, following)
+    )(blend, middle, following)
     return out.reshape(ensemble.shape)
 
 

time: 48.9 us -> 48.6 us (level)
  no operation moved by 1% of the time
where the time goes in v9:
time: 48.6 us; the launch traced here: 48.4 us
  Pallas kernels  48.4 us (100%)
    pallas_call x1, Pallas kernels, shards(): pl.pallas_call(first_kernel, out_shape=(jax.ShapeDtypeStruct((ROWS, K), B...  43.6 us
    pallas_call x1, Pallas kernels, shards(): pl.pallas_call(last_kernel, out_shape=jax.ShapeDtypeStruct((ROWS, K), BF1...  4.8 us

profile of v9, /device:TPU:1, one launch (start us, length us, event | category | flops | bytes accessed | tf_op | source)
XLA Modules:
  0.0 48.4 jit_solution(1978346740772000526)
XLA Ops:
  0.0 43.6 %analyse.1 = (bf16[24576,128]{1,0:T(8,128)(2,1)S(1)}, bf16[9,80,128]{2,1,0:T(8,128)(2,1)S(1)}, f32[384,128]{1,0:T(8,128)S(1)}) custom-call(s32[8,16]{1,0:T(8,128)} %count_any.1, s32[1,2048]{1,0:T(1,128)} %bitcast.6, f32[1,2048]{1,0:T(1,128)} %bitcast.7, f32[1,2048]{1,0:T(1,128)} %bitcast.8, bf16[24576,128]{1,0:T(8,128)(2,1)} %bitcast.5), custom_call_target="tpu_custom_call" | custom-call | tf_op jit(solution)/shard_map/analyse/pallas_call | solution.py:433
  43.6 4.8 %blend.1 = bf16[24576,128]{1,0:T(8,128)(2,1)} custom-call(bf16[9,80,128]{2,1,0:T(8,128)(2,1)S(1)} %get-tuple-element.8.nearby, f32[384,128]{1,0:T(8,128)S(1)} %get-tuple-element.9.middle, bf16[24576,128]{1,0:T(8,128)(2,1)S(1)} %get-tuple-element.10.ens), custom_call_target="tpu_custom_call" | custom-call | tf_op jit(solution)/shard_map/blend/pallas_call | solution.py:488

commit v10 on v9

--- a/solution.py
+++ b/solution.py
@@ -14,12 +14,12 @@
 OBS = 2048
 NEWTON = 6
 ITERS = 2
-QUART = 512
+QUART = 1024
 PART = 256
 GROUP = 8
 UNROLL = 4
 SLOTS = 4
-GATHER = 64
+GATHER = 128
 PACKED = 80
 BX = 8
 BY = 16
@@ -36,6 +36,14 @@
     return (a + 1) * 3 + (b + 1)
 
 
+def place_of(slot):
+    return (3, 4, 5, 0, 1, 2, 6, 7, 8)[slot]
+
+
+def lanes_of(slot):
+    return slice(place_of(slot) * K, place_of(slot) * K + K)
+
+
 def mm(a, b):
     return jnp.dot(a, b, preferred_element_type=F32)
 
@@ -59,6 +67,13 @@
     both = wide(b)
     out = mm(wide(a), jnp.concatenate([both, both], axis=0))
     return out[:, :K] + out[:, K:]
+
+
+def times_late(a, b):
+    a_high, a_low = split(a)
+    b_high, b_low = split(b)
+    left = jnp.concatenate([a_high, a_low, a_high], axis=1)
+    return mm(left, jnp.concatenate([b_high, b_high, b_low], axis=0))
 
 
 def iotas(shape):
@@ -135,12 +150,12 @@
     correction = 1.5 * identity - 0.5 * root
     root, inverse = times(correction, root), correction
     for step in range(1, NEWTON - 1):
-        correction = 1.5 * identity - 0.5 * times(inverse, root)
+        correction = 1.5 * identity - 0.5 * times_late(inverse, root)
         root, inverse = times(correction, root), times(correction, inverse)
-    correction = 1.5 * identity - 0.5 * times(inverse, root)
+    correction = 1.5 * identity - 0.5 * times_late(inverse, root)
     carried = times(jnp.broadcast_to(projected, (16, K)), inverse)
-    carried, inverse = times(carried, correction), times(correction, inverse)
-    weights = times(carried, inverse)[0:1] / frobenius
+    carried, inverse = times_late(carried, correction), times(correction, inverse)
+    weights = times_late(carried, inverse)[0:1] / frobenius
     return jnp.sqrt((K - 1) / frobenius) * inverse, weights
 
 
@@ -214,7 +229,7 @@
     applied, blend_ref, middle_ref,
     count_ref, cell_ref, given, cells_ref, ens, ens32, picked, rows, deviations, scaled, matrices, stationary,
     stat_x, stat_y, got_x, got_y, nearby, transforms, own_ref,
-    small_sem, load_sem, own_sem, send_x, recv_x, send_y, recv_y, send_t, recv_t,
+    small_sem, load_sem, send_x, recv_x, send_y, recv_y, send_t, recv_t,
 ):
     gx, gy = lax.axis_index("gx"), lax.axis_index("gy")
     nx, ny = lax.axis_size("gx"), lax.axis_size("gy")
@@ -320,7 +335,7 @@
         else:
             for q in range(OBS // QUART):
                 lanes = slice(q * QUART, (q + 1) * QUART)
-                fresh = rows[2:3, lanes] + mm(transforms[...], scaled[:, lanes])
+                fresh = deviations[:, lanes] + mm(transforms[:, 3 * K :], scaled[3 * K :, lanes])
                 fresh = fresh.astype(BF16).astype(F32)
                 centre = jnp.sum(fresh, axis=0, keepdims=True) * (1.0 / K)
                 total = accumulate(total, lanes, fresh - centre, centre)
@@ -334,7 +349,7 @@
             copy.start()
         if t == 1:
             for slot in range(9):
-                matrices[slot * K : (slot + 1) * K] = full_matrices(transforms[:, slot * K : (slot + 1) * K])
+                matrices[slot * K : (slot + 1) * K] = full_matrices(transforms[:, lanes_of(slot)])
             apply_some(0, CX // 2)
             settle()
         own = weighted(t, own, got_x, copies)
@@ -362,38 +377,39 @@
             copy.start()
         own = slot_of(0, 0)
         if t == 0:
-            transforms[:, own * K : (own + 1) * K] = (weights + spread).astype(BF16)
+            transforms[:, lanes_of(own)] = (weights + spread).astype(BF16)
 
             @pl.loop(0, OBS // PART)
             def _(q):
                 lanes = pl.ds(pl.multiple_of(q * PART, PART), PART)
                 for slot in range(9):
                     part = rows[3 + slot : 4 + slot, lanes] * deviations[:, lanes]
-                    scaled[slot * K : (slot + 1) * K, lanes] = part.astype(BF16)
+                    scaled[lanes_of(slot), lanes] = part.astype(BF16)
 
         else:
-            mine = pltpu.make_async_copy(own_ref.at[t], landing.at[own], own_sem)
-            mine.start()
             settle()
+            middle_ref[K : 2 * K] = full_matrices((weights + spread).astype(BF16))
         near, far = BLEND_STEPS[6:], BLEND_STEPS[:6]
         for step in near:
             copies[step].wait_recv()
-        if t == 1:
-            mine.wait()
-            middle_ref[K : 2 * K] = full_matrices((weights + spread).astype(BF16))
         for step in near:
             slot = slot_of(*step)
             if t == 0:
-                transforms[:, slot * K : (slot + 1) * K] = unpack_transform(nearby[slot])
+                transforms[:, lanes_of(slot)] = unpack_transform(nearby[slot])
             else:
                 here = (step[1] + 1) * K
                 middle_ref[here : here + K] = full_matrices(unpack_transform(blend_ref[slot]))
+        if t == 0:
+            for q in range(OBS // QUART):
+                lanes = slice(q * QUART, (q + 1) * QUART)
+                part = mm(transforms[:, : 3 * K], scaled[: 3 * K, lanes])
+                deviations[:, lanes] = rows[2:3, lanes] + part
         for step in far:
             copies[step].wait_recv()
         if t == 0:
             for step in far:
                 slot = slot_of(*step)
-                transforms[:, slot * K : (slot + 1) * K] = unpack_transform(nearby[slot])
+                transforms[:, lanes_of(slot)] = unpack_transform(nearby[slot])
         pending.extend(copies.values())
     settle()
 
@@ -461,7 +477,6 @@
             pltpu.VMEM((ITERS, PACKED, K), BF16),
             dma((5,)),
             dma((CX,)),
-            dma(()),
             dma((ITERS, 4)),
             dma((ITERS, 4)),
             dma((ITERS, 4)),

time: 48.6 us -> 48.5 us (level)
  no operation moved by 1% of the time
where the time goes in v10:
time: 48.5 us; the launch traced here: 48.4 us
  Pallas kernels  48.4 us (100%)
    pallas_call x1, Pallas kernels, shards(): pl.pallas_call(first_kernel, out_shape=(jax.ShapeDtypeStruct((ROWS, K), B...  43.6 us
    pallas_call x1, Pallas kernels, shards(): pl.pallas_call(last_kernel, out_shape=jax.ShapeDtypeStruct((ROWS, K), BF1...  4.81 us

profile of v10, /device:TPU:1, one launch (start us, length us, event | category | flops | bytes accessed | tf_op | source)
XLA Modules:
  0.0 48.4 jit_solution(16359558847271944035)
XLA Ops:
  0.0 43.6 %analyse.1 = (bf16[24576,128]{1,0:T(8,128)(2,1)S(1)}, bf16[9,80,128]{2,1,0:T(8,128)(2,1)S(1)}, f32[384,128]{1,0:T(8,128)S(1)}) custom-call(s32[8,16]{1,0:T(8,128)} %count_any.1, s32[1,2048]{1,0:T(1,128)} %bitcast.6, f32[1,2048]{1,0:T(1,128)} %bitcast.7, f32[1,2048]{1,0:T(1,128)} %bitcast.8, bf16[24576,128]{1,0:T(8,128)(2,1)} %bitcast.5), custom_call_target="tpu_custom_call" | custom-call | tf_op jit(solution)/shard_map/analyse/pallas_call | solution.py:449
  43.6 4.8 %blend.1 = bf16[24576,128]{1,0:T(8,128)(2,1)} custom-call(bf16[9,80,128]{2,1,0:T(8,128)(2,1)S(1)} %get-tuple-element.8.nearby, f32[384,128]{1,0:T(8,128)S(1)} %get-tuple-element.9.middle, bf16[24576,128]{1,0:T(8,128)(2,1)S(1)} %get-tuple-element.10.ens), custom_call_target="tpu_custom_call" | custom-call | tf_op jit(solution)/shard_map/blend/pallas_call | solution.py:503

commit v11 on v10

--- a/solution.py
+++ b/solution.py
@@ -260,15 +260,9 @@
     for copy in small:
         copy.wait()
     count = count_ref[gx, gy]
-    cells = cells_ref[...].astype(F32)
     slot = lax.broadcasted_iota(jnp.int32, (1, OBS), 1)
     rows[0:1] = jnp.where(slot < count, given[1], 0.0)
     rows[1:2] = given[0]
-    east = jnp.floor((cells + 0.5) * (1.0 / XROWS))
-    north = jnp.floor((cells - XROWS * east + 0.5) * (1.0 / LEV))
-    hat_x, hat_y = hats((east + 0.5) / CX), hats((north + 0.5) / CY)
-    for slot in range(9):
-        rows[3 + slot : 4 + slot] = hat_x[slot // 3] * hat_y[slot % 3]
 
     @pl.loop(0, CX)
     def _(i):
@@ -347,6 +341,13 @@
         copies = exchange(t, stat_x, got_x, send_x, recv_x, lambda step: (step, 0))
         for copy in copies:
             copy.start()
+        if t == 0:
+            cells = cells_ref[...].astype(F32)
+            column_x = jnp.floor((cells + 0.5) * (1.0 / XROWS))
+            column_y = jnp.floor((cells - XROWS * column_x + 0.5) * (1.0 / LEV))
+            hat_x, hat_y = hats((column_x + 0.5) / CX), hats((column_y + 0.5) / CY)
+            for slot in range(9):
+                rows[3 + slot : 4 + slot] = hat_x[slot // 3] * hat_y[slot % 3]
         if t == 1:
             for slot in range(9):
                 matrices[slot * K : (slot + 1) * K] = full_matrices(transforms[:, lanes_of(slot)])

time: 48.5 us -> 48.5 us (level)
  no operation moved by 1% of the time
where the time goes in v11:
time: 48.5 us; the launch traced here: 48.4 us
  Pallas kernels  48.4 us (100%)
    pallas_call x1, Pallas kernels, shards(): pl.pallas_call(first_kernel, out_shape=(jax.ShapeDtypeStruct((ROWS, K), B...  43.6 us
    pallas_call x1, Pallas kernels, shards(): pl.pallas_call(last_kernel, out_shape=jax.ShapeDtypeStruct((ROWS, K), BF1...  4.81 us

profile of v11, /device:TPU:1, one launch (start us, length us, event | category | flops | bytes accessed | tf_op | source)
XLA Modules:
  0.0 48.4 jit_solution(10913834125759129870)
XLA Ops:
  0.0 43.6 %analyse.1 = (bf16[24576,128]{1,0:T(8,128)(2,1)S(1)}, bf16[9,80,128]{2,1,0:T(8,128)(2,1)S(1)}, f32[384,128]{1,0:T(8,128)S(1)}) custom-call(s32[8,16]{1,0:T(8,128)} %count_any.1, s32[1,2048]{1,0:T(1,128)} %bitcast.6, f32[1,2048]{1,0:T(1,128)} %bitcast.7, f32[1,2048]{1,0:T(1,128)} %bitcast.8, bf16[24576,128]{1,0:T(8,128)(2,1)} %bitcast.5), custom_call_target="tpu_custom_call" | custom-call | tf_op jit(solution)/shard_map/analyse/pallas_call | solution.py:450
  43.6 4.8 %blend.1 = bf16[24576,128]{1,0:T(8,128)(2,1)} custom-call(bf16[9,80,128]{2,1,0:T(8,128)(2,1)S(1)} %get-tuple-element.8.nearby, f32[384,128]{1,0:T(8,128)S(1)} %get-tuple-element.9.middle, bf16[24576,128]{1,0:T(8,128)(2,1)S(1)} %get-tuple-element.10.ens), custom_call_target="tpu_custom_call" | custom-call | tf_op jit(solution)/shard_map/blend/pallas_call | solution.py:504
